TPU v7x, 256 devices: a whole 4x4x8 slice. The times are simulated.
256 devices in a mesh: ctx: 64 (over z, y, core), tp: 4 (over x).
Axes of the slice: x: 4, y: 4, z: 8, core: 2. Of those that a mesh axis runs over, the one named last changes fastest.
Arguments:
- queries: bfloat16 [16384, 64, 128], P('ctx', 'tp'), may hold values from -4 to 4
- keys: bfloat16 [16384, 8, 128], P('ctx', 'tp'), may hold values from -4 to 4
- values: bfloat16 [16384, 8, 128], P('ctx', 'tp'), may hold values from -6 to 6
- attn_out: bfloat16 [16384, 64, 128], P('ctx', 'tp'), may hold values from -6 to 6
- grad_out: bfloat16 [16384, 64, 128], P('ctx', 'tp'), may hold values from -4 to 4
- log_norm: float32 [64, 16384], P('tp', 'ctx'), may hold values from 2 to 4
- doc_lengths: int32 [32], replicated, may hold values from 1 to 1024, 16384 in all
- doc_weight: int32 [32], replicated, may hold values from 4 to 22
Outputs:
- grad_queries: float32 [16384, 64, 128], P('ctx', 'tp')
- grad_keys: float32 [16384, 8, 128], P('ctx', 'tp')
- grad_values: float32 [16384, 8, 128], P('ctx', 'tp')
Inputs may be any that keep to these rules, and one draw needn't show every extreme that they name: doc_lengths sum to 16384; the longest document has exactly 1024 tokens.
All inputs are finite; a program needn't handle non-finite values.
Results may differ from a plain program's by a relative error of at most 0.0041.
Values may be sent and summed in bfloat16 or wider, within the bound.
A program may use at most 128 MiB of HBM per device.

v0:
```python
import jax
import jax.numpy as jnp
from jax import lax
from jax.sharding import PartitionSpec as P

SPAN = 4


def from_behind(shard, axis, by):
    count = lax.axis_size(axis)
    pairs = [(i, i + by) for i in range(count) if 0 <= i + by < count]
    return lax.ppermute(shard, axis, pairs)


def doc_index(positions, doc_ends):
    counts = jnp.sum((positions[:, None] >= doc_ends[None, :]).astype(jnp.int32), axis=1)
    return jnp.where(positions >= 0, counts, -1)


def shards(queries, keys, values, attn_out, grad_out, log_norm, doc_lengths, doc_weight):
    tok_dev = queries.shape[0]
    head_dim = queries.shape[2]
    kv_dev = keys.shape[1]
    group_size = queries.shape[1] // kv_dev
    doc_count = doc_lengths.shape[0]
    ctx_count = lax.axis_size("ctx")
    shard_index = lax.axis_index("ctx")
    score_scale = head_dim ** (-0.5)
    doc_ends = jnp.cumsum(doc_lengths)
    local_rows = jnp.arange(tok_dev, dtype=jnp.int32)
    q_pos = shard_index * tok_dev + local_rows
    q_docs = doc_index(q_pos, doc_ends)
    matches = q_docs[:, None] == jnp.arange(doc_count, dtype=jnp.int32)[None, :]
    token_weight = jnp.sum(jnp.where(matches, doc_weight[None, :], 0), axis=1).astype(jnp.float32)
    weight_total = jnp.sum(doc_lengths * doc_weight).astype(jnp.float32)
    token_scale = token_weight * (tok_dev * ctx_count) / weight_total
    row_delta = token_scale[:, None] * jnp.sum(
        grad_out.astype(jnp.float32) * attn_out.astype(jnp.float32), axis=-1
    )
    delta_heads = row_delta.T.reshape(kv_dev, group_size, tok_dev)
    scaled_grad = (grad_out.astype(jnp.float32) * token_scale[:, None, None]).astype(jnp.bfloat16)
    query_heads = queries.reshape(tok_dev, kv_dev, group_size, head_dim)
    grad_heads = scaled_grad.reshape(tok_dev, kv_dev, group_size, head_dim)
    norm_heads = log_norm.reshape(kv_dev, group_size, tok_dev)

    def tile_grads(key_blk, value_blk, offset):
        k_pos = (shard_index - offset) * tok_dev + local_rows
        k_docs = doc_index(k_pos, doc_ends)
        allowed = (q_docs[:, None] == k_docs[None, :]) & (k_pos[None, :] <= q_pos[:, None])
        scores = (
            jnp.einsum("ihgd,jhd->hgij", query_heads, key_blk, preferred_element_type=jnp.float32)
            * score_scale
        )
        prob_full = jnp.where(allowed, jnp.exp(scores - norm_heads[..., None]), 0.0)
        prob_low = prob_full.astype(jnp.bfloat16)
        grad_v = jnp.einsum(
            "hgij,ihgd->jhd", prob_low, grad_heads, preferred_element_type=jnp.float32
        )
        grad_prob = jnp.einsum(
            "ihgd,jhd->hgij", grad_heads, value_blk, preferred_element_type=jnp.float32
        )
        grad_score = (prob_full * (grad_prob - delta_heads[..., None])).astype(jnp.bfloat16)
        grad_q = (
            jnp.einsum("hgij,jhd->ihgd", grad_score, key_blk, preferred_element_type=jnp.float32)
            * score_scale
        )
        grad_k = (
            jnp.einsum(
                "hgij,ihgd->jhd", grad_score, query_heads, preferred_element_type=jnp.float32
            )
            * score_scale
        )
        return (grad_q, grad_k, grad_v)

    grad_q_total, grad_k_own, grad_v_own = tile_grads(keys, values, 0)
    key_pair = jnp.stack([keys, values])
    grad_pair = jnp.stack([grad_k_own, grad_v_own])
    for offset in range(1, SPAN + 1):
        arrived = from_behind(key_pair, "ctx", offset)
        grad_q_part, grad_k_part, grad_v_part = tile_grads(arrived[0], arrived[1], offset)
        grad_q_total = grad_q_total + grad_q_part
        returned = from_behind(jnp.stack([grad_k_part, grad_v_part]), "ctx", -offset)
        grad_pair = grad_pair + returned
    return (
        grad_q_total.reshape(tok_dev, kv_dev * group_size, head_dim),
        grad_pair[0],
        grad_pair[1],
    )


def solution(mesh):
    return jax.shard_map(
        shards,
        mesh=mesh,
        in_specs=(
            P("ctx", "tp", None),
            P("ctx", "tp", None),
            P("ctx", "tp", None),
            P("ctx", "tp", None),
            P("ctx", "tp", None),
            P("tp", "ctx"),
            P(),
            P(),
        ),
        out_specs=(P("ctx", "tp", None), P("ctx", "tp", None), P("ctx", "tp", None)),
        check_vma=False,
    )
```

profile of v0, /device:TPU:229, one launch (start us, length us, event | category | flops | bytes accessed | tf_op | source)
XLA Modules:
  0.0 126.8 jit_solution(2415707755015592141)
XLA Ops:
  0.6 1.1 copy_bitcast_fusion
  1.8 3.8 %collective-permute-start = (bf16[2,256,2,128]{3,1,2,0:T(8,128)(2,1)S(1)}, bf16[2,256,2,128]{3,1,2,0:T(8,128)(2,1)S(1)}, u32[]{:S(2)}, u32[]{:S(2)}) collective-permute-start(bf16[2,256,2,128]{3,1,2,0:T(8,128)(2,1)S(1)} %pad_maximum_fusion.4), channel_id=1, source_target_pairs={{0,4},{4,8},{8,12},{12,16},{16,20},{20,24},{24,28},{28,32},{32,36}... | collective-permute-start | bytes 786440 | tf_op jit(solution)/shard_map/ppermute | solution.py:12
  5.5 3.2 %collective-permute-start.1 = (bf16[2,256,2,128]{3,1,2,0:T(8,128)(2,1)S(1)}, bf16[2,256,2,128]{3,1,2,0:T(8,128)(2,1)}, u32[]{:S(2)}, u32[]{:S(2)}) collective-permute-start(bf16[2,256,2,128]{3,1,2,0:T(8,128)(2,1)S(1)} %pad_maximum_fusion.4), channel_id=1, source_target_pairs={{0,8},{4,12},{8,16},{12,20},{16,24},{20,28},{24,32},{28,36},{32,40... | collective-permute-start | bytes 786440 | tf_op jit(solution)/shard_map/ppermute | solution.py:12
  8.8 3.5 %collective-permute-start.2 = (bf16[2,256,2,128]{3,1,2,0:T(8,128)(2,1)S(1)}, bf16[2,256,2,128]{3,1,2,0:T(8,128)(2,1)}, u32[]{:S(2)}, u32[]{:S(2)}) collective-permute-start(bf16[2,256,2,128]{3,1,2,0:T(8,128)(2,1)S(1)} %pad_maximum_fusion.4), channel_id=1, source_target_pairs={{0,12},{4,16},{8,20},{12,24},{16,28},{20,32},{24,36},{28,40},{32,4... | collective-permute-start | bytes 786440 | tf_op jit(solution)/shard_map/ppermute | solution.py:12
  12.3 1.9 %collective-permute-start.3 = (bf16[2,256,2,128]{3,1,2,0:T(8,128)(2,1)S(1)}, bf16[2,256,2,128]{3,1,2,0:T(8,128)(2,1)S(1)}, u32[]{:S(2)}, u32[]{:S(2)}) collective-permute-start(bf16[2,256,2,128]{3,1,2,0:T(8,128)(2,1)S(1)} %pad_maximum_fusion.4), channel_id=1, source_target_pairs={{0,16},{4,20},{8,24},{12,28},{16,32},{20,36},{24,40},{28,44},{32,4... | collective-permute-start | bytes 786440 | tf_op jit(solution)/shard_map/ppermute | solution.py:12
  15.3 1.3 %multiply_reduce_fusion = s32[]{:T(128)} fusion(s32[32]{0:T(128)} %param.14, s32[32]{0:T(128)} %param.15), kind=kLoop, calls=%fused_computation.126 | loop fusion | flops 63 | bytes 260 | tf_op jit(solution)/shard_map/reduce_sum | solution.py:35
  16.6 0.7 select_reduce_fusion
  18.1 2.6 %fusion.37 = (bf16[256,2,8,128]{3,2,1,0:T(8,128)(2,1)S(1)}, f32[256,16]{1,0:T(8,128)S(1)}) fusion(bf16[256,16,128]{2,1,0:T(8,128)(2,1)} %param.12, f32[256]{0:T(256)S(1)} %multiply_divide_fusion, bf16[256,16,128]{2,1,0:T(8,128)(2,1)} %param.11), kind=kLoop, calls=%fused_computation.63 | loop fusion | flops 3141632 | bytes 3163136 | tf_op jit(solution)/shard_map/reshape | solution.py:43
  22.1 1.8 %fusion.49 = f32[2,256,256,8]{2,1,3,0:T(8,128)S(1)} fusion(bf16[2,256,2,128]{3,1,2,0:T(8,128)(2,1)} %collective-permute-done.1, bf16[256,2,8,128]{3,2,1,0:T(8,128)(2,1)S(1)} %bitcast.297), kind=kOutput, calls=%fused_computation.99 | convolution fusion | flops 268435456 | bytes 5373952 | tf_op jit(solution)/shard_map/ihgd,jhd->hgij/dot_general | solution.py:51
  23.9 2.7 %collective-permute-done.2 = bf16[2,256,2,128]{3,1,2,0:T(8,128)(2,1)} collective-permute-done((bf16[2,256,2,128]{3,1,2,0:T(8,128)(2,1)S(1)}, bf16[2,256,2,128]{3,1,2,0:T(8,128)(2,1)}, u32[]{:S(2)}, u32[]{:S(2)}) %collective-permute-start.2) | collective-permute-done | bytes 262176 | tf_op jit(solution)/shard_map/ppermute | solution.py:12
  26.6 1.6 %fusion.51 = f32[2,256,256,8]{2,1,3,0:T(8,128)S(1)} fusion(bf16[2,256,2,128]{3,1,2,0:T(8,128)(2,1)} %collective-permute-done.2, bf16[256,2,8,128]{3,2,1,0:T(8,128)(2,1)S(1)} %bitcast.296), kind=kOutput, calls=%fused_computation.101 | convolution fusion | flops 268435456 | bytes 5373952 | tf_op jit(solution)/shard_map/ihgd,jhd->hgij/dot_general | solution.py:51
  29.2 1.0 copy-done.1
  30.2 6.2 %fusion.20 = (bf16[2,8,256,256]{2,3,1,0:T(8,128)(2,1)}, bf16[2,8,256,256]{2,3,1,0:T(8,128)(2,1)}, bf16[2,8,256,256]{2,3,1,0:T(8,128)(2,1)}, bf16[2,8,256,256]{2,...) fusion(f32[2,8,256]{2,1,0:T(8,128)S(1)} %bitcast.303, ...), kind=kOutput, calls=%fused_computation.30 | convolution fusion | flops 289406976 | bytes 32980992 | tf_op jit(solution)/shard_map/ihgd,jhd->hgij/dot_general | solution.py:51
  36.4 4.6 %copy.250 = bf16[2,8,256,256]{3,1,0,2:T(8,128)(2,1)} copy(bf16[2,8,256,256]{2,3,1,0:T(8,128)(2,1)} %get-tuple-element.28) | data formatting | bytes 4194304 | tf_op jit(solution)/shard_map/convert_element_type | solution.py:55
  41.0 2.5 %convolution_bitcast_fusion.6 = f32[1,256,2,128]{3,1,2,0:T(8,128)S(1)} fusion(bf16[256,2,8,128]{3,2,1,0:T(8,128)(2,1)S(1)} %get-tuple-element.23, bf16[2,8,256,256]{3,1,0,2:T(8,128)(2,1)} %copy.250), kind=kOutput, calls=%fused_computation.52 | convolution fusion | flops 268435456 | bytes 3407872 | tf_op jit(solution)/shard_map/hgij,ihgd->jhd/dot_general | solution.py:56
  43.6 3.6 %fusion.13 = bf16[2,8,256,256]{2,3,1,0:T(8,128)(2,1)S(1)} fusion(f32[2,256,256,8]{2,1,3,0:T(8,128)} %copy-done.4, f32[2,8,256]{2,1,0:T(8,128)S(1)} %bitcast.309, f32[2,8,256]{2,1,0:T(8,128)S(1)} %bitcast.304, pred[256,256]{0,1:T(8,128)(4,1)S(1)} %get-tuple-element.35, bf16[256,2,8,128]{3,2,1,0:T(8,128)(2,1)S(1)} %get-tuple-element.23, ...), kind=kOutput, calls=%fused_computation.20 | convolution fusion | flops 274726912 | bytes 7569408 | tf_op jit(solution)/shard_map/ihgd,jhd->hgij/dot_general | solution.py:59
  48.6 2.1 %collective-permute-start.4 = (f32[2,256,2,128]{3,1,2,0:T(8,128)S(1)}, f32[2,256,2,128]{3,1,2,0:T(8,128)}, u32[]{:S(2)}, u32[]{:S(2)}) collective-permute-start(f32[2,256,2,128]{3,1,2,0:T(8,128)S(1)} %pad_maximum_fusion), channel_id=1, source_target_pairs={{4,0},{8,4},{12,8},{16,12},{20,16},{24,20},{28,24},{32,28},{36,32}... | collective-permute-start | bytes 1572872 | tf_op jit(solution)/shard_map/ppermute | solution.py:12
  50.7 4.5 %copy.253 = bf16[2,8,256,256]{3,1,0,2:T(8,128)(2,1)} copy(bf16[2,8,256,256]{2,3,1,0:T(8,128)(2,1)} %get-tuple-element.29) | data formatting | bytes 4194304 | tf_op jit(solution)/shard_map/convert_element_type | solution.py:55
  55.2 2.5 %convolution_bitcast_fusion.4 = f32[1,256,2,128]{3,1,2,0:T(8,128)S(1)} fusion(bf16[256,2,8,128]{3,2,1,0:T(8,128)(2,1)S(1)} %get-tuple-element.23, bf16[2,8,256,256]{3,1,0,2:T(8,128)(2,1)} %copy.253), kind=kOutput, calls=%fused_computation.49 | convolution fusion | flops 268435456 | bytes 3407872 | tf_op jit(solution)/shard_map/hgij,ihgd->jhd/dot_general | solution.py:56
  57.7 3.7 %fusion.9 = bf16[2,8,256,256]{2,3,1,0:T(8,128)(2,1)S(1)} fusion(f32[2,256,256,8]{2,1,3,0:T(8,128)} %copy-done.3, f32[2,8,256]{2,1,0:T(8,128)S(1)} %bitcast.310, f32[2,8,256]{2,1,0:T(8,128)S(1)} %bitcast.305, pred[256,256]{0,1:T(8,128)(4,1)S(1)} %get-tuple-element.36, bf16[256,2,8,128]{3,2,1,0:T(8,128)(2,1)S(1)} %get-tuple-element.23, ...), kind=kOutput, calls=%fused_computation.14 | convolution fusion | flops 274726912 | bytes 7569408 | tf_op jit(solution)/shard_map/ihgd,jhd->hgij/dot_general | solution.py:59
  61.4 0.8 fusion.34
  62.7 4.9 %collective-permute-start.5 = (f32[2,256,2,128]{3,1,2,0:T(8,128)S(1)}, f32[2,256,2,128]{3,1,2,0:T(8,128)}, u32[]{:S(2)}, u32[]{:S(2)}) collective-permute-start(f32[2,256,2,128]{3,1,2,0:T(8,128)S(1)} %pad_maximum_fusion.1), channel_id=1, source_target_pairs={{8,0},{12,4},{16,8},{20,12},{24,16},{28,20},{32,24},{36,28},{40,32... | collective-permute-start | bytes 1572872 | tf_op jit(solution)/shard_map/ppermute | solution.py:12
  67.6 4.5 %copy.259 = bf16[2,8,256,256]{3,1,0,2:T(8,128)(2,1)} copy(bf16[2,8,256,256]{2,3,1,0:T(8,128)(2,1)} %get-tuple-element.31) | data formatting | bytes 4194304 | tf_op jit(solution)/shard_map/convert_element_type | solution.py:55
  72.1 2.5 %convolution_bitcast_fusion = f32[1,256,2,128]{3,1,2,0:T(8,128)S(1)} fusion(bf16[256,2,8,128]{3,2,1,0:T(8,128)(2,1)S(1)} %get-tuple-element.23, bf16[2,8,256,256]{3,1,0,2:T(8,128)(2,1)} %copy.259), kind=kOutput, calls=%fused_computation.43 | convolution fusion | flops 268435456 | bytes 3407872 | tf_op jit(solution)/shard_map/hgij,ihgd->jhd/dot_general | solution.py:56
  74.7 3.7 %fusion.1 = bf16[2,8,256,256]{2,3,1,0:T(8,128)(2,1)S(1)} fusion(f32[2,256,256,8]{2,1,3,0:T(8,128)} %copy-done.2, f32[2,8,256]{2,1,0:T(8,128)S(1)} %bitcast.311, f32[2,8,256]{2,1,0:T(8,128)S(1)} %bitcast.306, pred[256,256]{0,1:T(8,128)(4,1)S(1)} %get-tuple-element.32, bf16[256,2,8,128]{3,2,1,0:T(8,128)(2,1)S(1)} %get-tuple-element.23, ...), kind=kOutput, calls=%fused_computation.2 | convolution fusion | flops 274726912 | bytes 7569408 | tf_op jit(solution)/shard_map/ihgd,jhd->hgij/dot_general | solution.py:59
  78.4 0.7 fusion.36
  79.1 0.8 pad_maximum_fusion.3
  79.9 4.1 %collective-permute-start.7 = (f32[2,256,2,128]{3,1,2,0:T(8,128)}, f32[2,256,2,128]{3,1,2,0:T(8,128)}, u32[]{:S(2)}, u32[]{:S(2)}) collective-permute-start(f32[2,256,2,128]{3,1,2,0:T(8,128)} %pad_maximum_fusion.3), channel_id=1, source_target_pairs={{16,0},{20,4},{24,8},{28,12},{32,16},{36,20},{40,24},{44,28},{48,3... | collective-permute-start | bytes 1572872 | tf_op jit(solution)/shard_map/ppermute | solution.py:12
  84.0 4.5 %copy.256 = bf16[2,8,256,256]{3,1,0,2:T(8,128)(2,1)} copy(bf16[2,8,256,256]{2,3,1,0:T(8,128)(2,1)} %get-tuple-element.30) | data formatting | bytes 4194304 | tf_op jit(solution)/shard_map/convert_element_type | solution.py:55
  88.5 2.5 %convolution_bitcast_fusion.2 = f32[1,256,2,128]{3,1,2,0:T(8,128)S(1)} fusion(bf16[256,2,8,128]{3,2,1,0:T(8,128)(2,1)S(1)} %get-tuple-element.23, bf16[2,8,256,256]{3,1,0,2:T(8,128)(2,1)} %copy.256), kind=kOutput, calls=%fused_computation.46 | convolution fusion | flops 268435456 | bytes 3407872 | tf_op jit(solution)/shard_map/hgij,ihgd->jhd/dot_general | solution.py:56
  91.0 3.7 %fusion.5 = bf16[2,8,256,256]{2,3,1,0:T(8,128)(2,1)S(1)} fusion(f32[2,256,256,8]{2,1,3,0:T(8,128)} %copy-done.1, f32[2,8,256]{2,1,0:T(8,128)S(1)} %bitcast.312, f32[2,8,256]{2,1,0:T(8,128)S(1)} %bitcast.307, pred[256,256]{0,1:T(8,128)(4,1)S(1)} %get-tuple-element.33, bf16[256,2,8,128]{3,2,1,0:T(8,128)(2,1)S(1)} %get-tuple-element.23, ...), kind=kOutput, calls=%fused_computation.8 | convolution fusion | flops 274726912 | bytes 7569408 | tf_op jit(solution)/shard_map/ihgd,jhd->hgij/dot_general | solution.py:59
  94.8 0.8 fusion.35
  95.5 0.8 pad_maximum_fusion.2
  96.4 5.1 %collective-permute-start.6 = (f32[2,256,2,128]{3,1,2,0:T(8,128)}, f32[2,256,2,128]{3,1,2,0:T(8,128)}, u32[]{:S(2)}, u32[]{:S(2)}) collective-permute-start(f32[2,256,2,128]{3,1,2,0:T(8,128)} %pad_maximum_fusion.2), channel_id=1, source_target_pairs={{12,0},{16,4},{20,8},{24,12},{28,16},{32,20},{36,24},{40,28},{44,3... | collective-permute-start | bytes 1572872 | tf_op jit(solution)/shard_map/ppermute | solution.py:12
  101.5 4.6 %copy.247 = bf16[2,8,256,256]{3,1,0,2:T(8,128)(2,1)} copy(bf16[2,8,256,256]{2,3,1,0:T(8,128)(2,1)} %get-tuple-element.27) | data formatting | bytes 4194304 | tf_op jit(solution)/shard_map/convert_element_type | solution.py:55
  106.1 3.6 %fusion.17 = bf16[2,8,256,256]{2,3,1,0:T(8,128)(2,1)S(1)} fusion(f32[2,256,256,8]{2,1,3,0:T(8,128)} %get-tuple-element.37, f32[2,8,256]{2,1,0:T(8,128)S(1)} %bitcast.313, f32[2,8,256]{2,1,0:T(8,128)S(1)} %bitcast.308, pred[256,256]{0,1:T(8,128)(4,1)S(1)} %get-tuple-element.34, bf16[256,2,8,128]{3,2,1,0:T(8,128)(2,1)S(1)} %get-tuple-element.23, ...), kind=kOutput, calls=%fused_computation.26 | convolution fusion | flops 274726912 | bytes 7569408 | tf_op jit(solution)/shard_map/ihgd,jhd->hgij/dot_general | solution.py:59
  109.7 0.9 fusion.54
  111.3 0.9 fusion.48
  112.9 2.0 %fusion.50 = f32[2,128,8,256]{1,3,2,0:T(8,128)S(1)} fusion(bf16[2,8,256,256]{2,3,1,0:T(8,128)(2,1)S(1)} %copy-done.11, bf16[2,256,2,128]{3,1,2,0:T(8,128)(2,1)} %collective-permute-done.1), kind=kOutput, calls=%fused_computation.100 | convolution fusion | flops 268435456 | bytes 4325376 | tf_op jit(solution)/shard_map/hgij,jhd->ihgd/dot_general | solution.py:64
  114.9 2.0 %fusion.52 = f32[2,128,8,256]{1,3,2,0:T(8,128)S(1)} fusion(bf16[2,8,256,256]{2,3,1,0:T(8,128)(2,1)S(1)} %copy-done.13, bf16[2,256,2,128]{3,1,2,0:T(8,128)(2,1)} %collective-permute-done.2), kind=kOutput, calls=%fused_computation.102 | convolution fusion | flops 268435456 | bytes 4325376 | tf_op jit(solution)/shard_map/hgij,jhd->ihgd/dot_general | solution.py:64
  116.9 1.2 bitcast_add_fusion
  118.2 2.5 %copy.261 = f32[256,16,128]{2,1,0:T(8,128)} copy(f32[256,16,128]{2,0,1:T(8,128)S(1)} %bitcast.299) | data formatting | bytes 4194304
  120.7 0.7 fusion.32
  121.4 0.8 copy-done.5
  122.3 0.9 convolution_bitcast_fusion.8
  123.3 1.7 %fusion.45 = f32[2,256,2,128]{3,1,2,0:T(8,128)S(1)} fusion(f32[2,256,2,128]{3,1,2,0:T(8,128)} %collective-permute-done.7, f32[2,256,2,128]{3,1,2,0:T(8,128)} %collective-permute-done.6, f32[2,256,2,128]{3,1,2,0:T(8,128)} %collective-permute-done.5, f32[2,256,2,128]{3,1,2,0:T(8,128)} %collective-permute-done.4, ...), kind=kLoop, calls=%fused_computation.72 | loop fusion | flops 655360 | bytes 3145728 | tf_op jit(solution)/shard_map/add | solution.py:83
  125.0 0.9 copy.262
  125.9 0.9 copy.263
  (72 shorter events, 6.7 us)
Async XLA Ops:
  0.6 20.7 %copy-start = (bf16[256,16,128]{2,1,0:T(8,128)(2,1)S(1)}, bf16[256,16,128]{2,1,0:T(8,128)(2,1)}, u32[]{:S(2)}) copy-start(bf16[256,16,128]{2,1,0:T(8,128)(2,1)} %param.8) | copy-start | bytes 3145732
  1.8 19.6 %collective-permute-start = (bf16[2,256,2,128]{3,1,2,0:T(8,128)(2,1)S(1)}, bf16[2,256,2,128]{3,1,2,0:T(8,128)(2,1)S(1)}, u32[]{:S(2)}, u32[]{:S(2)}) collective-permute-start(bf16[2,256,2,128]{3,1,2,0:T(8,128)(2,1)S(1)} %pad_maximum_fusion.4), channel_id=1, source_target_pairs={{0,4},{4,8},{8,12},{12,16},{16,20},{20,24},{24,28},{28,32},{32,36}... | collective-permute-start | bytes 786440 | tf_op jit(solution)/shard_map/ppermute | solution.py:12
  5.5 16.6 %collective-permute-start.1 = (bf16[2,256,2,128]{3,1,2,0:T(8,128)(2,1)S(1)}, bf16[2,256,2,128]{3,1,2,0:T(8,128)(2,1)}, u32[]{:S(2)}, u32[]{:S(2)}) collective-permute-start(bf16[2,256,2,128]{3,1,2,0:T(8,128)(2,1)S(1)} %pad_maximum_fusion.4), channel_id=1, source_target_pairs={{0,8},{4,12},{8,16},{12,20},{16,24},{20,28},{24,32},{28,36},{32,40... | collective-permute-start | bytes 786440 | tf_op jit(solution)/shard_map/ppermute | solution.py:12
  8.8 17.8 %collective-permute-start.2 = (bf16[2,256,2,128]{3,1,2,0:T(8,128)(2,1)S(1)}, bf16[2,256,2,128]{3,1,2,0:T(8,128)(2,1)}, u32[]{:S(2)}, u32[]{:S(2)}) collective-permute-start(bf16[2,256,2,128]{3,1,2,0:T(8,128)(2,1)S(1)} %pad_maximum_fusion.4), channel_id=1, source_target_pairs={{0,12},{4,16},{8,20},{12,24},{16,28},{20,32},{24,36},{28,40},{32,4... | collective-permute-start | bytes 786440 | tf_op jit(solution)/shard_map/ppermute | solution.py:12
  12.3 16.0 %collective-permute-start.3 = (bf16[2,256,2,128]{3,1,2,0:T(8,128)(2,1)S(1)}, bf16[2,256,2,128]{3,1,2,0:T(8,128)(2,1)S(1)}, u32[]{:S(2)}, u32[]{:S(2)}) collective-permute-start(bf16[2,256,2,128]{3,1,2,0:T(8,128)(2,1)S(1)} %pad_maximum_fusion.4), channel_id=1, source_target_pairs={{0,16},{4,20},{8,24},{12,28},{16,32},{20,36},{24,40},{28,44},{32,4... | collective-permute-start | bytes 786440 | tf_op jit(solution)/shard_map/ppermute | solution.py:12
  21.4 22.2 %copy-start.18 = (bf16[2,256,2,128]{3,1,2,0:T(8,128)(2,1)}, bf16[2,256,2,128]{3,1,2,0:T(8,128)(2,1)S(1)}, u32[]{:S(2)}) copy-start(bf16[2,256,2,128]{3,1,2,0:T(8,128)(2,1)S(1)} %collective-permute-done) | copy-start | bytes 786436
  22.1 7.1 %copy-start.4 = (f32[2,256,256,8]{2,1,3,0:T(8,128)}, f32[2,256,256,8]{2,1,3,0:T(8,128)S(1)}, u32[]{:S(2)}) copy-start(f32[2,256,256,8]{2,1,3,0:T(8,128)S(1)} %fusion.47) | copy-start | bytes 12582916
  23.9 5.3 %copy-start.3 = (f32[2,256,256,8]{2,1,3,0:T(8,128)}, f32[2,256,256,8]{2,1,3,0:T(8,128)S(1)}, u32[]{:S(2)}) copy-start(f32[2,256,256,8]{2,1,3,0:T(8,128)S(1)} %fusion.49) | copy-start | bytes 12582916
  28.2 2.0 %copy-start.1 = (f32[2,256,256,8]{2,1,3,0:T(8,128)}, f32[2,256,256,8]{2,1,3,0:T(8,128)S(1)}, u32[]{:S(2)}) copy-start(f32[2,256,256,8]{2,1,3,0:T(8,128)S(1)} %fusion.51) | copy-start | bytes 12582916
  28.2 2.0 %copy-start.14 = (bf16[256,2,128]{2,1,0:T(2,128)(2,1)S(1)}, bf16[256,2,128]{2,1,0:T(2,128)(2,1)}, u32[]{:S(2)}) copy-start(bf16[256,2,128]{2,1,0:T(2,128)(2,1)} %param.9) | copy-start | bytes 393220
  28.2 2.0 %copy-start.21 = (f32[16,256]{1,0:T(8,128)S(1)}, f32[16,256]{1,0:T(8,128)}, u32[]{:S(2)}) copy-start(f32[16,256]{1,0:T(8,128)} %param.13) | copy-start | bytes 49156
  28.3 0.9 copy-start.15
  29.2 7.2 %copy-start.2 = (f32[2,256,256,8]{2,1,3,0:T(8,128)}, f32[2,256,256,8]{2,1,3,0:T(8,128)S(1)}, u32[]{:S(2)}) copy-start(f32[2,256,256,8]{2,1,3,0:T(8,128)S(1)} %fusion.53) | copy-start | bytes 12582916
  47.2 1.3 %copy-start.8 = (bf16[2,8,256,256]{2,3,1,0:T(8,128)(2,1)}, bf16[2,8,256,256]{2,3,1,0:T(8,128)(2,1)S(1)}, u32[]{:S(2)}) copy-start(bf16[2,8,256,256]{2,3,1,0:T(8,128)(2,1)S(1)} %fusion.13) | copy-start | bytes 6291460
  48.6 74.7 %collective-permute-start.4 = (f32[2,256,2,128]{3,1,2,0:T(8,128)S(1)}, f32[2,256,2,128]{3,1,2,0:T(8,128)}, u32[]{:S(2)}, u32[]{:S(2)}) collective-permute-start(f32[2,256,2,128]{3,1,2,0:T(8,128)S(1)} %pad_maximum_fusion), channel_id=1, source_target_pairs={{4,0},{8,4},{12,8},{16,12},{20,16},{24,20},{28,24},{32,28},{36,32}... | collective-permute-start | bytes 1572872 | tf_op jit(solution)/shard_map/ppermute | solution.py:12
  61.4 1.3 %copy-start.10 = (bf16[2,8,256,256]{2,3,1,0:T(8,128)(2,1)}, bf16[2,8,256,256]{2,3,1,0:T(8,128)(2,1)S(1)}, u32[]{:S(2)}) copy-start(bf16[2,8,256,256]{2,3,1,0:T(8,128)(2,1)S(1)} %fusion.9) | copy-start | bytes 6291460
  62.7 60.6 %collective-permute-start.5 = (f32[2,256,2,128]{3,1,2,0:T(8,128)S(1)}, f32[2,256,2,128]{3,1,2,0:T(8,128)}, u32[]{:S(2)}, u32[]{:S(2)}) collective-permute-start(f32[2,256,2,128]{3,1,2,0:T(8,128)S(1)} %pad_maximum_fusion.1), channel_id=1, source_target_pairs={{8,0},{12,4},{16,8},{20,12},{24,16},{28,20},{32,24},{36,28},{40,32... | collective-permute-start | bytes 1572872 | tf_op jit(solution)/shard_map/ppermute | solution.py:12
  72.1 2.6 %copy-start.16 = (bf16[2,256,2,128]{3,1,2,0:T(8,128)(2,1)S(1)}, bf16[2,256,2,128]{3,1,2,0:T(8,128)(2,1)}, u32[]{:S(2)}) copy-start(bf16[2,256,2,128]{3,1,2,0:T(8,128)(2,1)} %copy-done.15) | copy-start | bytes 786436
  78.3 1.6 %copy-start.6 = (bf16[2,8,256,256]{2,3,1,0:T(8,128)(2,1)}, bf16[2,8,256,256]{2,3,1,0:T(8,128)(2,1)S(1)}, u32[]{:S(2)}) copy-start(bf16[2,8,256,256]{2,3,1,0:T(8,128)(2,1)S(1)} %fusion.1) | copy-start | bytes 6291460
  79.9 43.3 %collective-permute-start.7 = (f32[2,256,2,128]{3,1,2,0:T(8,128)}, f32[2,256,2,128]{3,1,2,0:T(8,128)}, u32[]{:S(2)}, u32[]{:S(2)}) collective-permute-start(f32[2,256,2,128]{3,1,2,0:T(8,128)} %pad_maximum_fusion.3), channel_id=1, source_target_pairs={{16,0},{20,4},{24,8},{28,12},{32,16},{36,20},{40,24},{44,28},{48,3... | collective-permute-start | bytes 1572872 | tf_op jit(solution)/shard_map/ppermute | solution.py:12
  94.8 1.6 %copy-start.12 = (bf16[2,8,256,256]{2,3,1,0:T(8,128)(2,1)}, bf16[2,8,256,256]{2,3,1,0:T(8,128)(2,1)S(1)}, u32[]{:S(2)}) copy-start(bf16[2,8,256,256]{2,3,1,0:T(8,128)(2,1)S(1)} %fusion.5) | copy-start | bytes 6291460
  96.4 26.9 %collective-permute-start.6 = (f32[2,256,2,128]{3,1,2,0:T(8,128)}, f32[2,256,2,128]{3,1,2,0:T(8,128)}, u32[]{:S(2)}, u32[]{:S(2)}) collective-permute-start(f32[2,256,2,128]{3,1,2,0:T(8,128)} %pad_maximum_fusion.2), channel_id=1, source_target_pairs={{12,0},{16,4},{20,8},{24,12},{28,16},{32,20},{36,24},{40,28},{44,3... | collective-permute-start | bytes 1572872 | tf_op jit(solution)/shard_map/ppermute | solution.py:12
  101.5 4.6 %copy-start.20 = (bf16[256,2,128]{2,1,0:T(2,128)(2,1)S(1)}, bf16[256,2,128]{2,1,0:T(2,128)(2,1)}, u32[]{:S(2)}) copy-start(bf16[256,2,128]{2,1,0:T(2,128)(2,1)} %param.10) | copy-start | bytes 393220
  109.7 1.6 %copy-start.9 = (bf16[2,8,256,256]{2,3,1,0:T(8,128)(2,1)S(1)}, bf16[2,8,256,256]{2,3,1,0:T(8,128)(2,1)}, u32[]{:S(2)}) copy-start(bf16[2,8,256,256]{2,3,1,0:T(8,128)(2,1)} %copy-done.8) | copy-start | bytes 6291460
  109.7 1.6 %copy-start.19 = (bf16[2,256,2,128]{3,1,2,0:T(8,128)(2,1)S(1)}, bf16[2,256,2,128]{3,1,2,0:T(8,128)(2,1)}, u32[]{:S(2)}) copy-start(bf16[2,256,2,128]{3,1,2,0:T(8,128)(2,1)} %copy-done.18) | copy-start | bytes 786436
  111.3 1.6 %copy-start.11 = (bf16[2,8,256,256]{2,3,1,0:T(8,128)(2,1)S(1)}, bf16[2,8,256,256]{2,3,1,0:T(8,128)(2,1)}, u32[]{:S(2)}) copy-start(bf16[2,8,256,256]{2,3,1,0:T(8,128)(2,1)} %copy-done.10) | copy-start | bytes 6291460
  112.9 2.0 %copy-start.13 = (bf16[2,8,256,256]{2,3,1,0:T(8,128)(2,1)S(1)}, bf16[2,8,256,256]{2,3,1,0:T(8,128)(2,1)}, u32[]{:S(2)}) copy-start(bf16[2,8,256,256]{2,3,1,0:T(8,128)(2,1)} %copy-done.12) | copy-start | bytes 6291460
  114.9 2.0 %copy-start.7 = (bf16[2,8,256,256]{2,3,1,0:T(8,128)(2,1)S(1)}, bf16[2,8,256,256]{2,3,1,0:T(8,128)(2,1)}, u32[]{:S(2)}) copy-start(bf16[2,8,256,256]{2,3,1,0:T(8,128)(2,1)} %copy-done.6) | copy-start | bytes 6291460
  114.9 2.0 %copy-start.17 = (bf16[2,256,2,128]{3,1,2,0:T(8,128)(2,1)S(1)}, bf16[2,256,2,128]{3,1,2,0:T(8,128)(2,1)}, u32[]{:S(2)}) copy-start(bf16[2,256,2,128]{3,1,2,0:T(8,128)(2,1)} %copy-done.15) | copy-start | bytes 786436
  120.7 1.6 %copy-start.5 = (bf16[2,8,256,256]{3,1,0,2:T(8,128)(2,1)S(1)}, bf16[2,8,256,256]{3,1,0,2:T(8,128)(2,1)}, u32[]{:S(2)}) copy-start(bf16[2,8,256,256]{3,1,0,2:T(8,128)(2,1)} %copy.247) | copy-start | bytes 6291460
where the time goes:
time: 128 us; the launch traced here: 127 us
  matrix products  51.2 us (40%)
  local copies, waits for them, and re-layouts  33.4 us (26%)
  starting transfers between devices  28.6 us (22%)
  other arithmetic  9.06 us (7%)
  waiting for transfers between devices  2.69 us (2%)
  between operations  1.9 us (1%)
    ppermute x8, starting transfers between devices, from_behind(): return lax.ppermute(shard, axis, pairs)  28.6 us
    convert_element_type x5, local copies, waits for them, and re-layouts, tile_grads(): prob_low = prob_full.astype(jnp.bfloat16)  22.7 us
    dot_general x5, matrix products, tile_grads(): jnp.einsum('ihgd,jhd->hgij', grad_heads, value_blk, preferred_element_typ...  18.4 us
    dot_general x5, matrix products, tile_grads(): jnp.einsum('ihgd,jhd->hgij', query_heads, key_blk, preferred_element_type...  11 us
    dot_general x5, matrix products, tile_grads(): jnp.einsum('hgij,ihgd->jhd', prob_low, grad_heads, preferred_element_type...  11 us
    unnamed x47, local copies, waits for them, and re-layouts  8.81 us
    dot_general x5, matrix products, tile_grads(): jnp.einsum('hgij,jhd->ihgd', grad_score, key_blk, preferred_element_type=...  7.04 us
    dot_general x5, matrix products, tile_grads(): jnp.einsum('hgij,ihgd->jhd', grad_score, query_heads, preferred_element_t...  3.74 us
  transfers between devices with their start and end apart: 8, of which 1 were waited for; matrix products, arithmetic and copies ran while one was open for 52% of the time, Pallas kernels for 0%

commit v1 on v0

v1 whole, which is shorter than its diff:
```python
import functools

import jax
import jax.numpy as jnp
from jax import lax
from jax.experimental import pallas as pl
from jax.experimental.pallas import tpu as pltpu
from jax.sharding import PartitionSpec as P

MESH = pl.DeviceIdType.MESH
F32, BF16 = jnp.float32, jnp.bfloat16
NT = (((1,), (1,)), ((), ()))
NN = (((1,), (0,)), ((), ()))

TOK = 256
HD = 128
GROUP = 8
DOCS = 32
SCALE = HD ** -0.5
DOC_LANE = 64
FAR_AWAY = 16384.0


def dot(a, b, dims):
    return lax.dot_general(a, b, dims, preferred_element_type=F32)


def iota(shape, dim):
    return lax.broadcasted_iota(jnp.int32, shape, dim)


def kernel(n_ctx, q_hbm, k_hbm, v_hbm, o_hbm, g_hbm, ln_hbm, dl_ref, dw_ref, dq_ref, dk_ref, dv_ref,
           q_in, k_in, v_in, o_in, g_in, ln_in,
           kv_send, kvs, kaug, q_all, g_all, a_all, q_s, g_s, a_s, xaug, yaug, qt, gt, go_hi, go_lo,
           p_buf, d_buf, own_part, mate_part, ret_send, ret_recv, dq_send, dq_hm, totals,
           in_sem, kv_ssem, kv_rsem, x_ssem, x_rsem, r_ssem, r_rsem, m_ssem, m_rsem, dq_ssem, dq_rsem):
    me = lax.axis_index("ctx")
    tp = lax.axis_index("tp")
    core = lax.rem(me, 2)
    chip2 = me - core
    mate = chip2 + 1 - core

    def at(chips, j):
        return (lax.rem(chip2 + 2 * chips + j + n_ctx, n_ctx), tp)

    def remote(src, dst, ssem, rsem, dev):
        return pltpu.make_async_remote_copy(src_ref=src, dst_ref=dst, send_sem=ssem, recv_sem=rsem,
                                            device_id=dev, device_id_type=MESH)

    mate_dev = (mate, tp)
    loads = [pltpu.make_async_copy(s, d, in_sem.at[i]) for i, (s, d) in enumerate(
        [(k_hbm, k_in), (v_hbm, v_in), (g_hbm, g_in), (o_hbm, o_in), (q_hbm, q_in), (ln_hbm, ln_in)])]
    for load in loads:
        load.start()
    barrier = pltpu.get_barrier_semaphore()
    peers = [mate_dev] + [at(d, j) for d in (1, -1, 2, -2) for j in (0, 1)]
    for peer in peers:
        pl.semaphore_signal(barrier, inc=1, device_id=peer, device_id_type=MESH)

    loads[0].wait()
    kv_send[:, 0] = jnp.swapaxes(k_in[...], 0, 1)
    loads[1].wait()
    kv_send[:, 1] = jnp.swapaxes(v_in[...], 0, 1)
    kvs[4 + core] = kv_send[core]
    pl.semaphore_wait(barrier, len(peers))

    sends = [remote(kv_send.at[1 - core], kvs.at[4 + core], kv_ssem.at[0], kv_rsem.at[4 + core], mate_dev)]
    for i, (chips, slot) in enumerate(((1, 2), (2, 0))):
        for h in (0, 1):
            sends.append(remote(kv_send.at[h], kvs.at[slot + core], kv_ssem.at[1 + 2 * i + h],
                                kv_rsem.at[slot + core], at(chips, h)))
    for s in sends:
        s.start()

    def wait_block(kb):
        remote(kv_send.at[0], kvs.at[kb], kv_ssem.at[0], kv_rsem.at[kb], mate_dev).wait_recv()

    def wait_return(i):
        remote(ret_send.at[0, 0], ret_recv.at[i], r_ssem.at[0], r_rsem.at[i], mate_dev).wait_recv()

    lane1 = iota((1, HD), 1)
    starts = jnp.full((1, HD), 1 << 30, jnp.int32)
    ends = jnp.zeros((1, HD), jnp.int32)
    weights = jnp.zeros((1, HD), F32)
    run = jnp.int32(0)
    total = jnp.int32(0)
    for d in range(DOCS):
        here = lane1 == DOC_LANE + d
        length = dl_ref[d]
        weight = dw_ref[d]
        starts = jnp.where(here, run, starts)
        run = run + length
        ends = jnp.where(here, run, ends)
        weights = jnp.where(here, weight.astype(F32), weights)
        total = total + length * weight

    rows = iota((TOK, HD), 0)
    lanes = iota((TOK, HD), 1)

    def one_hot(block):
        pos = block * TOK + rows
        return (pos >= starts) & (pos < ends)

    for kb in range(6):
        hot = one_hot(chip2 - 4 + kb)
        extra = jnp.where(lanes < 48, 1.0, jnp.where((lanes >= DOC_LANE) & (lanes < DOC_LANE + DOCS) & ~hot, -FAR_AWAY, 0.0))
        kaug[kb] = extra.astype(BF16)

    scale = jnp.sum(jnp.where(one_hot(me), weights, 0.0), axis=1, keepdims=True)
    scale = scale * float(n_ctx * TOK) / total.astype(F32)
    scale = jnp.broadcast_to(scale, (TOK, HD))

    loads[2].wait()
    g_all[...] = jnp.swapaxes(g_in[...], 0, 1)
    loads[3].wait()
    q_all[...] = jnp.swapaxes(o_in[...], 0, 1)
    for h in range(2 * GROUP):
        g = g_all[h].astype(F32)
        go = g * q_all[h].astype(F32)
        hi = go.astype(BF16)
        cols = pl.ds(h * HD, HD)
        go_hi[:, cols] = hi
        go_lo[:, cols] = (go - hi.astype(F32)).astype(BF16)
        g_all[h] = (g * scale).astype(BF16)
    send_g = remote(g_all.at[pl.ds(GROUP * (1 - core), GROUP)], g_s.at[core], x_ssem.at[0], x_rsem.at[0], mate_dev)
    send_g.start()
    loads[4].wait()
    q_all[...] = jnp.swapaxes(q_in[...], 0, 1)
    send_q = remote(q_all.at[pl.ds(GROUP * (1 - core), GROUP)], q_s.at[core], x_ssem.at[1], x_rsem.at[1], mate_dev)
    send_q.start()
    g_s[core] = g_all[pl.ds(GROUP * core, GROUP)]
    q_s[core] = q_all[pl.ds(GROUP * core, GROUP)]

    big = iota((2 * GROUP * HD, HD), 0) // HD
    bl = iota((2 * GROUP * HD, HD), 1)
    pick = jnp.where((bl >= DOC_LANE) & (bl < DOC_LANE + 48) & (lax.rem(bl, 16) == big), 1.0, 0.0).astype(BF16)
    delta = dot(go_hi[...], pick, NN) + dot(go_lo[...], pick, NN)
    loads[5].wait()
    ln = ln_in[...]
    norm = jnp.concatenate([ln, ln, ln, jnp.zeros((80, TOK), F32)], axis=0).T
    z = jnp.where(lanes < 48, norm * (-(HD ** 0.5)), -(delta * scale))
    hi = z.astype(BF16)
    rest = z - hi.astype(F32)
    mid = rest.astype(BF16)
    low = (rest - mid.astype(F32)).astype(BF16)
    term = lax.rem(lanes, 64) // 16
    a_all[...] = jnp.where(term == 0, hi.astype(F32), jnp.where(term == 1, mid.astype(F32), low.astype(F32))).astype(BF16)
    send_a = remote(a_all, a_s.at[core], x_ssem.at[2], x_rsem.at[2], mate_dev)
    send_a.start()
    a_s[core] = a_all[...]

    def prepare(qb):
        a = a_s[qb].astype(F32)
        hot = one_hot(chip2 + qb)
        base = jnp.where(hot, 1.0, 0.0)
        slot = lax.rem(lanes, 16)
        for g in range(GROUP):
            mine = slot == GROUP * core + g
            xaug[qb, g] = jnp.where(mine & (lanes < 48), a, base).astype(BF16)
            yaug[qb, g] = jnp.where(mine & (lanes >= 64) & (lanes < 112), a, 0.0).astype(BF16)
            cols = pl.ds(pl.multiple_of((qb * GROUP + g) * TOK, TOK), TOK)
            qt[:, cols] = q_s[qb, g].T
            gt[:, cols] = g_s[qb, g].T

    ones = jnp.ones((TOK, HD), BF16)

    def keys_of(kbs):
        return jnp.concatenate([jnp.concatenate([kvs[kb, 0], kaug[kb]], axis=1) for kb in kbs], axis=0)

    def values_of(kbs):
        return jnp.concatenate([jnp.concatenate([kvs[kb, 1], ones], axis=1) for kb in kbs], axis=0)

    causal = iota((TOK, TOK), 0) >= iota((TOK, TOK), 1)

    def scores(qb, kbs, diagonal=False):
        width = TOK * len(kbs)
        cols = pl.ds(kbs[0] * TOK, width)
        keys, values = keys_of(kbs), values_of(kbs)
        for g in range(GROUP):
            x = jnp.concatenate([q_s[qb, g], xaug[qb, g]], axis=1)
            y = jnp.concatenate([g_s[qb, g], yaug[qb, g]], axis=1)
            p = jnp.exp(dot(x, keys, NT) * SCALE)
            if diagonal:
                keep = causal if len(kbs) == 1 else jnp.concatenate([jnp.ones((TOK, TOK), jnp.bool_), causal], axis=1)
                p = jnp.where(keep, p, 0.0)
            ds = p * dot(y, values, NT)
            at_rows = pl.ds((qb * GROUP + g) * TOK, TOK)
            p_buf[at_rows, cols] = p.astype(BF16)
            d_buf[at_rows, cols] = ds.astype(BF16)

    half = GROUP * TOK

    def kv_grads(first_row, kb, count):
        r = pl.ds(first_row, 2 * half - first_row) if first_row else slice(None)
        c = pl.ds(kb * TOK, count * TOK)
        return dot(qt[:, r], d_buf[r, c], NN), dot(gt[:, r], p_buf[r, c], NN)

    prepare(core)
    wait_block(5 - core)
    for s in (send_g, send_q, send_a):
        s.wait_recv()
    prepare(1 - core)

    scores(0, (4,), True)
    scores(1, (4, 5), True)
    dk0, dv0 = kv_grads(0, 4, 1)
    dk1, dv1 = kv_grads(half, 5, 1)
    own_part[0, 0] = dk0
    own_part[0, 1] = dv0
    own_part[1, 0] = dk1
    own_part[1, 1] = dv1
    send_m = remote(own_part.at[1 - core], mate_part, m_ssem.at[0], m_rsem.at[0], mate_dev)
    send_m.start()

    def give_back(stage, slot, chips):
        out = []
        for j in (0, 1):
            c = remote(ret_send.at[stage, j], ret_recv.at[slot + core], r_ssem.at[2 * stage + j], r_rsem.at[slot + core],
                       at(chips, j))
            c.start()
            out.append(c)
        return out

    wait_block(2)
    wait_block(3)
    scores(0, (2, 3))
    scores(1, (2, 3))
    dk, dv = kv_grads(0, 2, 2)
    for j in (0, 1):
        ret_send[0, j, 0] = dk[:, j * TOK:(j + 1) * TOK].astype(BF16)
        ret_send[0, j, 1] = dv[:, j * TOK:(j + 1) * TOK].astype(BF16)
    returns = give_back(0, 0, -1)

    wait_block(0)
    wait_block(1)
    scores(0, (0, 1))
    scores(1, (1,))
    r0 = pl.ds(0, half)
    c0 = pl.ds(0, TOK)
    ret_send[1, 0, 0] = dot(qt[:, r0], d_buf[r0, c0], NN).astype(BF16)
    ret_send[1, 0, 1] = dot(gt[:, r0], p_buf[r0, c0], NN).astype(BF16)
    dk, dv = kv_grads(0, 1, 1)
    ret_send[1, 1, 0] = dk.astype(BF16)
    ret_send[1, 1, 1] = dv.astype(BF16)
    returns += give_back(1, 2, -2)

    def query_grads(qb, out_at):
        keys = kvs[pl.ds(qb, 5), 0].reshape(5 * TOK, HD)
        for g in range(GROUP):
            r = pl.ds(pl.multiple_of((qb * GROUP + g) * TOK, TOK), TOK)
            c = pl.ds(pl.multiple_of(qb * TOK, TOK), 5 * TOK)
            out_at(g, dot(d_buf[r, c], keys, NN) * SCALE)

    def to_mate(g, x):
        dq_send[g] = x

    def to_own(g, x):
        dq_hm[GROUP * core + g] = x

    query_grads(1 - core, to_mate)
    send_dq = remote(dq_send, dq_hm.at[pl.ds(GROUP * core, GROUP)], dq_ssem.at[0], dq_rsem.at[0], mate_dev)
    send_dq.start()
    query_grads(core, to_own)
    send_dq.wait_recv()
    dq_ref[...] = jnp.swapaxes(dq_hm[...], 0, 1)

    send_m.wait_recv()
    for i in range(4):
        wait_return(i)

    def add_up(part, h):
        x = part + ret_recv[h].astype(F32) + ret_recv[2 + h].astype(F32)
        totals[h, 0] = x[0].T * SCALE
        totals[h, 1] = x[1].T

    add_up(own_part[core], core)
    add_up(mate_part[...], 1 - core)
    dk_ref[...] = jnp.swapaxes(totals[:, 0], 0, 1)
    dv_ref[...] = jnp.swapaxes(totals[:, 1], 0, 1)
    for s in sends + [send_g, send_q, send_a, send_m, send_dq] + returns:
        s.wait_send()


def shards(n_ctx, queries, keys, values, attn_out, grad_out, log_norm, doc_lengths, doc_weight):
    any_space = pl.BlockSpec(memory_space=pl.ANY)
    smem = pl.BlockSpec(memory_space=pltpu.SMEM)
    vmem = pl.BlockSpec(memory_space=pltpu.VMEM)
    dma = pltpu.SemaphoreType.DMA
    q_shape, k_shape = queries.shape, keys.shape
    wide = 2 * GROUP * TOK

    def buf(*shape, dtype=BF16):
        return pltpu.VMEM(shape, dtype)

    return pl.pallas_call(
        functools.partial(kernel, n_ctx),
        out_shape=(
            jax.ShapeDtypeStruct(q_shape, F32),
            jax.ShapeDtypeStruct(k_shape, F32),
            jax.ShapeDtypeStruct(k_shape, F32),
        ),
        in_specs=[any_space] * 6 + [smem] * 2,
        out_specs=(vmem, vmem, vmem),
        scratch_shapes=[
            buf(*q_shape), buf(*k_shape), buf(*k_shape), buf(*q_shape), buf(*q_shape), buf(2 * GROUP, TOK, dtype=F32),
            buf(2, 2, TOK, HD), buf(6, 2, TOK, HD), buf(6, TOK, HD),
            buf(2 * GROUP, TOK, HD), buf(2 * GROUP, TOK, HD), buf(TOK, HD),
            buf(2, GROUP, TOK, HD), buf(2, GROUP, TOK, HD), buf(2, TOK, HD),
            buf(2, GROUP, TOK, HD), buf(2, GROUP, TOK, HD),
            buf(HD, wide), buf(HD, wide), buf(TOK, 2 * GROUP * HD), buf(TOK, 2 * GROUP * HD),
            buf(wide, 6 * TOK), buf(wide, 6 * TOK),
            buf(2, 2, HD, TOK, dtype=F32), buf(2, HD, TOK, dtype=F32),
            buf(2, 2, 2, HD, TOK), buf(4, 2, HD, TOK),
            buf(GROUP, TOK, HD, dtype=F32), buf(2 * GROUP, TOK, HD, dtype=F32), buf(2, 2, TOK, HD, dtype=F32),
            dma((6,)), dma((5,)), dma((6,)), dma((3,)), dma((3,)), dma((4,)), dma((4,)), dma((1,)), dma((1,)),
            dma((1,)), dma((1,)),
        ],
        compiler_params=pltpu.CompilerParams(collective_id=0, has_side_effects=True, vmem_limit_bytes=60 << 20),
    )(queries, keys, values, attn_out, grad_out, log_norm, doc_lengths, doc_weight)


def solution(mesh):
    return jax.shard_map(
        functools.partial(shards, mesh.shape["ctx"]),
        mesh=mesh,
        in_specs=(
            P("ctx", "tp", None),
            P("ctx", "tp", None),
            P("ctx", "tp", None),
            P("ctx", "tp", None),
            P("ctx", "tp", None),
            P("tp", "ctx"),
            P(),
            P(),
        ),
        out_specs=(P("ctx", "tp", None), P("ctx", "tp", None), P("ctx", "tp", None)),
        check_vma=False,
    )
```

time: 128 us -> 43.1 us (0.34)
  the two profiles are of different devices: /device:TPU:229 before, /device:TPU:13 now
where the time goes in v1:
time: 43.1 us; the launch traced here: 43 us
  Pallas kernels  37.8 us (88%)
  local copies, waits for them, and re-layouts  4.51 us (10%)
  between operations  0.66 us (2%)
    pallas_call x1, Pallas kernels, shards(): pl.pallas_call(functools.partial(kernel, n_ctx), out_shape=(jax.ShapeDtyp...  37.8 us
    unnamed x7, local copies, waits for them, and re-layouts  4.51 us

profile of v1, /device:TPU:13, one launch (start us, length us, event | category | flops | bytes accessed | tf_op | source)
XLA Modules:
  0.0 43.0 jit_solution(7931560963892467845)
XLA Ops:
  0.6 37.8 %shard_map.103 = (f32[256,16,128]{2,1,0:T(8,128)}, f32[256,2,128]{2,1,0:T(2,128)}, f32[256,2,128]{2,1,0:T(2,128)}) custom-call(bf16[256,16,128]{2,1,0:T(8,128)(2,1)} %q_hbm.1, bf16[256,2,128]{2,1,0:T(2,128)(2,1)} %k_hbm.1, bf16[256,2,128]{2,1,0:T(2,128)(2,1)} %v_hbm.1, bf16[256,16,128]{2,1,0:T(8,128)(2,1)} %o_hbm.1, bf16[256,16,128]{2,1,0:T(8,128)(2,1)} %g_hbm.1, ...), custom_call_target="tpu_custom_call" | custom-call | tf_op jit(solution)/shard_map/pallas_call | solution.py:295
  38.5 0.0 copy-start.1
  38.5 0.0 copy-start
  38.5 3.1 %copy.14 = f32[256,16,128]{2,1,0:T(8,128)} copy(f32[256,16,128]{2,1,0:T(8,128)} %get-tuple-element.6) | data formatting | bytes 4194304
  41.6 0.0 copy-done.1
  41.6 0.7 %copy.15 = f32[256,2,128]{2,1,0:T(2,128)} copy(f32[256,2,128]{2,1,0:T(2,128)S(1)} %copy-done.1) | data formatting | bytes 524288
  42.3 0.0 copy-done
  42.3 0.7 %copy.16 = f32[256,2,128]{2,1,0:T(2,128)} copy(f32[256,2,128]{2,1,0:T(2,128)S(1)} %copy-done) | data formatting | bytes 524288
Async XLA Ops:
  38.5 3.1 %copy-start.1 = (f32[256,2,128]{2,1,0:T(2,128)S(1)}, f32[256,2,128]{2,1,0:T(2,128)}, u32[]{:S(2)}) copy-start(f32[256,2,128]{2,1,0:T(2,128)} %get-tuple-element.7) | copy-start | bytes 786436
  38.5 3.8 %copy-start = (f32[256,2,128]{2,1,0:T(2,128)S(1)}, f32[256,2,128]{2,1,0:T(2,128)}, u32[]{:S(2)}) copy-start(f32[256,2,128]{2,1,0:T(2,128)} %get-tuple-element.8) | copy-start | bytes 786436

commit v2 on v1

--- a/solution.py
+++ b/solution.py
@@ -32,7 +32,7 @@
 def kernel(n_ctx, q_hbm, k_hbm, v_hbm, o_hbm, g_hbm, ln_hbm, dl_ref, dw_ref, dq_ref, dk_ref, dv_ref,
            q_in, k_in, v_in, o_in, g_in, ln_in,
            kv_send, kvs, kaug, q_all, g_all, a_all, q_s, g_s, a_s, xaug, yaug, qt, gt, go_hi, go_lo,
-           p_buf, d_buf, own_part, mate_part, ret_send, ret_recv, dq_send, dq_hm, totals,
+           p_buf, d_buf, own_part, mate_part, ret_send, ret_recv, dq_acc, dq_mate, totals,
            in_sem, kv_ssem, kv_rsem, x_ssem, x_rsem, r_ssem, r_rsem, m_ssem, m_rsem, dq_ssem, dq_rsem):
     me = lax.axis_index("ctx")
     tp = lax.axis_index("tp")
@@ -65,10 +65,8 @@
     pl.semaphore_wait(barrier, len(peers))
 
     sends = [remote(kv_send.at[1 - core], kvs.at[4 + core], kv_ssem.at[0], kv_rsem.at[4 + core], mate_dev)]
-    for i, (chips, slot) in enumerate(((1, 2), (2, 0))):
-        for h in (0, 1):
-            sends.append(remote(kv_send.at[h], kvs.at[slot + core], kv_ssem.at[1 + 2 * i + h],
-                                kv_rsem.at[slot + core], at(chips, h)))
+    for h in (0, 1):
+        sends.append(remote(kv_send.at[h], kvs.at[2 + core], kv_ssem.at[1 + h], kv_rsem.at[2 + core], at(1, h)))
     for s in sends:
         s.start()
 
@@ -76,7 +74,7 @@
         remote(kv_send.at[0], kvs.at[kb], kv_ssem.at[0], kv_rsem.at[kb], mate_dev).wait_recv()
 
     def wait_return(i):
-        remote(ret_send.at[0, 0], ret_recv.at[i], r_ssem.at[0], r_rsem.at[i], mate_dev).wait_recv()
+        remote(ret_send.at[0], ret_recv.at[i], r_ssem.at[0], r_rsem.at[i], mate_dev).wait_recv()
 
     lane1 = iota((1, HD), 1)
     starts = jnp.full((1, HD), 1 << 30, jnp.int32)
@@ -212,57 +210,53 @@
     send_m = remote(own_part.at[1 - core], mate_part, m_ssem.at[0], m_rsem.at[0], mate_dev)
     send_m.start()
 
-    def give_back(stage, slot, chips):
-        out = []
-        for j in (0, 1):
-            c = remote(ret_send.at[stage, j], ret_recv.at[slot + core], r_ssem.at[2 * stage + j], r_rsem.at[slot + core],
-                       at(chips, j))
-            c.start()
-            out.append(c)
-        return out
-
-    wait_block(2)
-    wait_block(3)
+    for j in (0, 1):
+        wait_block(2 + j)
+        onward = remote(kvs.at[2 + j], kvs.at[j], kv_ssem.at[3 + j], kv_rsem.at[j], at(1, core))
+        onward.start()
+        sends.append(onward)
+
+    returns = []
+
+    def give_back(i, j, chips, slot, dk, dv):
+        ret_send[i, 0] = dk.astype(BF16)
+        ret_send[i, 1] = dv.astype(BF16)
+        c = remote(ret_send.at[i], ret_recv.at[slot + core], r_ssem.at[i], r_rsem.at[slot + core], at(chips, j))
+        c.start()
+        returns.append(c)
+
     scores(0, (2, 3))
     scores(1, (2, 3))
     dk, dv = kv_grads(0, 2, 2)
     for j in (0, 1):
-        ret_send[0, j, 0] = dk[:, j * TOK:(j + 1) * TOK].astype(BF16)
-        ret_send[0, j, 1] = dv[:, j * TOK:(j + 1) * TOK].astype(BF16)
-    returns = give_back(0, 0, -1)
+        give_back(j, j, -1, 0, dk[:, j * TOK:(j + 1) * TOK], dv[:, j * TOK:(j + 1) * TOK])
+
+    def query_grads(qb, first, count):
+        keys = kvs[first:first + count, 0].reshape(count * TOK, HD)
+        return dot(d_buf[qb * half:(qb + 1) * half, first * TOK:(first + count) * TOK], keys, NN)
+
+    dq_acc[0] = query_grads(0, 2, 3).reshape(GROUP, TOK, HD)
+    dq_acc[1] = query_grads(1, 2, 4).reshape(GROUP, TOK, HD)
 
     wait_block(0)
-    wait_block(1)
-    scores(0, (0, 1))
-    scores(1, (1,))
+    scores(0, (0,))
     r0 = pl.ds(0, half)
     c0 = pl.ds(0, TOK)
-    ret_send[1, 0, 0] = dot(qt[:, r0], d_buf[r0, c0], NN).astype(BF16)
-    ret_send[1, 0, 1] = dot(gt[:, r0], p_buf[r0, c0], NN).astype(BF16)
-    dk, dv = kv_grads(0, 1, 1)
-    ret_send[1, 1, 0] = dk.astype(BF16)
-    ret_send[1, 1, 1] = dv.astype(BF16)
-    returns += give_back(1, 2, -2)
-
-    def query_grads(qb, out_at):
-        keys = kvs[pl.ds(qb, 5), 0].reshape(5 * TOK, HD)
-        for g in range(GROUP):
-            r = pl.ds(pl.multiple_of((qb * GROUP + g) * TOK, TOK), TOK)
-            c = pl.ds(pl.multiple_of(qb * TOK, TOK), 5 * TOK)
-            out_at(g, dot(d_buf[r, c], keys, NN) * SCALE)
-
-    def to_mate(g, x):
-        dq_send[g] = x
-
-    def to_own(g, x):
-        dq_hm[GROUP * core + g] = x
-
-    query_grads(1 - core, to_mate)
-    send_dq = remote(dq_send, dq_hm.at[pl.ds(GROUP * core, GROUP)], dq_ssem.at[0], dq_rsem.at[0], mate_dev)
+    give_back(2, 0, -2, 2, dot(qt[:, r0], d_buf[r0, c0], NN), dot(gt[:, r0], p_buf[r0, c0], NN))
+    wait_block(1)
+    scores(0, (1,))
+    scores(1, (1,))
+    give_back(3, 1, -2, 2, *kv_grads(0, 1, 1))
+
+    dq_acc[0] = (dq_acc[0] + query_grads(0, 0, 2).reshape(GROUP, TOK, HD)) * SCALE
+    dq_acc[1] = (dq_acc[1] + query_grads(1, 1, 1).reshape(GROUP, TOK, HD)) * SCALE
+    send_dq = remote(dq_acc.at[1 - core], dq_mate, dq_ssem.at[0], dq_rsem.at[0], mate_dev)
     send_dq.start()
-    query_grads(core, to_own)
     send_dq.wait_recv()
-    dq_ref[...] = jnp.swapaxes(dq_hm[...], 0, 1)
+    low = jnp.where(core == 0, dq_acc[core], dq_mate[...])
+    high = jnp.where(core == 0, dq_mate[...], dq_acc[core])
+    dq_ref[:, :GROUP] = jnp.swapaxes(low, 0, 1)
+    dq_ref[:, GROUP:] = jnp.swapaxes(high, 0, 1)
 
     send_m.wait_recv()
     for i in range(4):
@@ -270,13 +264,13 @@
 
     def add_up(part, h):
         x = part + ret_recv[h].astype(F32) + ret_recv[2 + h].astype(F32)
-        totals[h, 0] = x[0].T * SCALE
-        totals[h, 1] = x[1].T
+        totals[0, h] = x[0].T * SCALE
+        totals[1, h] = x[1].T
 
     add_up(own_part[core], core)
     add_up(mate_part[...], 1 - core)
-    dk_ref[...] = jnp.swapaxes(totals[:, 0], 0, 1)
-    dv_ref[...] = jnp.swapaxes(totals[:, 1], 0, 1)
+    dk_ref[...] = jnp.swapaxes(totals[0], 0, 1)
+    dv_ref[...] = jnp.swapaxes(totals[1], 0, 1)
     for s in sends + [send_g, send_q, send_a, send_m, send_dq] + returns:
         s.wait_send()
 
@@ -295,9 +289,9 @@
     return pl.pallas_call(
         functools.partial(kernel, n_ctx),
         out_shape=(
-            jax.ShapeDtypeStruct(q_shape, F32),
-            jax.ShapeDtypeStruct(k_shape, F32),
-            jax.ShapeDtypeStruct(k_shape, F32),
+            buf(*q_shape, dtype=F32),
+            buf(*k_shape, dtype=F32),
+            buf(*k_shape, dtype=F32),
         ),
         in_specs=[any_space] * 6 + [smem] * 2,
         out_specs=(vmem, vmem, vmem),
@@ -310,12 +304,12 @@
             buf(HD, wide), buf(HD, wide), buf(TOK, 2 * GROUP * HD), buf(TOK, 2 * GROUP * HD),
             buf(wide, 6 * TOK), buf(wide, 6 * TOK),
             buf(2, 2, HD, TOK, dtype=F32), buf(2, HD, TOK, dtype=F32),
-            buf(2, 2, 2, HD, TOK), buf(4, 2, HD, TOK),
-            buf(GROUP, TOK, HD, dtype=F32), buf(2 * GROUP, TOK, HD, dtype=F32), buf(2, 2, TOK, HD, dtype=F32),
+            buf(4, 2, HD, TOK), buf(4, 2, HD, TOK),
+            buf(2, GROUP, TOK, HD, dtype=F32), buf(GROUP, TOK, HD, dtype=F32), buf(2, 2, TOK, HD, dtype=F32),
             dma((6,)), dma((5,)), dma((6,)), dma((3,)), dma((3,)), dma((4,)), dma((4,)), dma((1,)), dma((1,)),
             dma((1,)), dma((1,)),
         ],
-        compiler_params=pltpu.CompilerParams(collective_id=0, has_side_effects=True, vmem_limit_bytes=60 << 20),
+        compiler_params=pltpu.CompilerParams(collective_id=0, has_side_effects=True, vmem_limit_bytes=52 << 20),
     )(queries, keys, values, attn_out, grad_out, log_norm, doc_lengths, doc_weight)
 
 

time: 43.1 us -> 38.3 us (0.89)
  the two profiles are of different devices: /device:TPU:13 before, /device:TPU:1 now
where the time goes in v2:
time: 38.3 us; the launch traced here: 38.2 us
  Pallas kernels  34.9 us (91%)
  local copies, waits for them, and re-layouts  2.73 us (7%)
  between operations  0.64 us (2%)
    pallas_call x1, Pallas kernels, shards(): pl.pallas_call(functools.partial(kernel, n_ctx), out_shape=(buf(*q_shape,...  34.9 us
    unnamed x3, local copies, waits for them, and re-layouts  2.73 us

profile of v2, /device:TPU:1, one launch (start us, length us, event | category | flops | bytes accessed | tf_op | source)
XLA Modules:
  0.0 38.2 jit_solution(17462410396325752611)
XLA Ops:
  0.6 34.9 %shard_map.103 = (f32[256,16,128]{2,1,0:T(8,128)S(1)}, f32[256,2,128]{2,1,0:T(2,128)S(1)}, f32[256,2,128]{2,1,0:T(2,128)S(1)}) custom-call(bf16[256,16,128]{2,1,0:T(8,128)(2,1)} %q_hbm.1, bf16[256,2,128]{2,1,0:T(2,128)(2,1)} %k_hbm.1, bf16[256,2,128]{2,1,0:T(2,128)(2,1)} %v_hbm.1, bf16[256,16,128]{2,1,0:T(8,128)(2,1)} %o_hbm.1, bf16[256,16,128]{2,1,0:T(8,128)(2,1)} %g_hbm.1, ...), custom_call_target="tpu_custom_call" | custom-call | tf_op jit(solution)/shard_map/pallas_call | solution.py:289
  35.5 1.3 %copy.14 = f32[256,16,128]{2,1,0:T(8,128)} copy(f32[256,16,128]{2,1,0:T(8,128)S(1)} %get-tuple-element.3) | data formatting | bytes 4194304
  36.8 0.7 %copy.15 = f32[256,2,128]{2,1,0:T(2,128)} copy(f32[256,2,128]{2,1,0:T(2,128)S(1)} %get-tuple-element.4) | data formatting | bytes 524288
  37.5 0.7 %copy.16 = f32[256,2,128]{2,1,0:T(2,128)} copy(f32[256,2,128]{2,1,0:T(2,128)S(1)} %get-tuple-element.5) | data formatting | bytes 524288

commit v3 on v2

--- a/solution.py
+++ b/solution.py
@@ -16,6 +16,7 @@
 HD = 128
 GROUP = 8
 DOCS = 32
+RING = 4
 SCALE = HD ** -0.5
 DOC_LANE = 64
 FAR_AWAY = 16384.0
@@ -31,14 +32,25 @@
 
 def kernel(n_ctx, q_hbm, k_hbm, v_hbm, o_hbm, g_hbm, ln_hbm, dl_ref, dw_ref, dq_ref, dk_ref, dv_ref,
            q_in, k_in, v_in, o_in, g_in, ln_in,
-           kv_send, kvs, kaug, q_all, g_all, a_all, q_s, g_s, a_s, xaug, yaug, qt, gt, go_hi, go_lo,
-           p_buf, d_buf, own_part, mate_part, ret_send, ret_recv, dq_acc, dq_mate, totals,
-           in_sem, kv_ssem, kv_rsem, x_ssem, x_rsem, r_ssem, r_rsem, m_ssem, m_rsem, dq_ssem, dq_rsem):
+           kv_send, kvs, kaug, q_all, g_all, a_all, q_s, g_s, a_s, xaug, yaug, qt, gt,
+           p_buf, d_buf, own_part, mate_part, ret_send, ret_recv, dq_send, dq_all, totals,
+           in_sem, kv_ssem, kv_rsem, x_ssem, x_rsem, r_ssem, r_rsem, m_ssem, m_rsem, dq_ssem, dq_rsem, hop, hop_ssem, hop_rsem):
     me = lax.axis_index("ctx")
     tp = lax.axis_index("tp")
     core = lax.rem(me, 2)
     chip2 = me - core
     mate = chip2 + 1 - core
+    before = {1: chip2 >= 2, 2: chip2 >= 4}
+    after = {1: chip2 < n_ctx - 2, 2: chip2 < n_ctx - 4}
+
+    chip = chip2 // 2
+    base, y = chip // RING * RING, lax.rem(chip, RING)
+    down, up = base + lax.rem(y + RING - 1, RING), base + lax.rem(y + 1, RING)
+    origin = lax.rem(chip + n_ctx // 2 - 2, n_ctx // 2)
+    relay = origin // RING * RING + lax.rem(origin + RING - 1, RING)
+    hop_from_here = after[2] & (core == 1)
+    hop_through_here = up + 2 < n_ctx // 2
+    hop_end = lax.rem(up + 2, n_ctx // 2)
 
     def at(chips, j):
         return (lax.rem(chip2 + 2 * chips + j + n_ctx, n_ctx), tp)
@@ -53,28 +65,31 @@
     for load in loads:
         load.start()
     barrier = pltpu.get_barrier_semaphore()
-    peers = [mate_dev] + [at(d, j) for d in (1, -1, 2, -2) for j in (0, 1)]
-    for peer in peers:
-        pl.semaphore_signal(barrier, inc=1, device_id=peer, device_id_type=MESH)
+    pl.semaphore_signal(barrier, inc=1, device_id=mate_dev, device_id_type=MESH)
+    greeted = 1
+    for chips, there in ((1, after[1]), (2, after[2]), (-1, before[1]), (-2, before[2])):
+        greeted = greeted + 2 * there.astype(jnp.int32)
+
+        @pl.when(there)
+        def _():
+            for j in (0, 1):
+                pl.semaphore_signal(barrier, inc=1, device_id=at(chips, j), device_id_type=MESH)
+
+    for there, devs in ((hop_from_here, [(2 * down, tp), (2 * down + 1, tp)]),
+                        (hop_through_here, [(2 * up + 1, tp), (2 * hop_end + core, tp)]),
+                        (before[2], [(2 * relay + core, tp)])):
+        greeted = greeted + len(devs) * there.astype(jnp.int32)
+
+        @pl.when(there)
+        def _():
+            for dev in devs:
+                pl.semaphore_signal(barrier, inc=1, device_id=dev, device_id_type=MESH)
 
     loads[0].wait()
     kv_send[:, 0] = jnp.swapaxes(k_in[...], 0, 1)
     loads[1].wait()
     kv_send[:, 1] = jnp.swapaxes(v_in[...], 0, 1)
     kvs[4 + core] = kv_send[core]
-    pl.semaphore_wait(barrier, len(peers))
-
-    sends = [remote(kv_send.at[1 - core], kvs.at[4 + core], kv_ssem.at[0], kv_rsem.at[4 + core], mate_dev)]
-    for h in (0, 1):
-        sends.append(remote(kv_send.at[h], kvs.at[2 + core], kv_ssem.at[1 + h], kv_rsem.at[2 + core], at(1, h)))
-    for s in sends:
-        s.start()
-
-    def wait_block(kb):
-        remote(kv_send.at[0], kvs.at[kb], kv_ssem.at[0], kv_rsem.at[kb], mate_dev).wait_recv()
-
-    def wait_return(i):
-        remote(ret_send.at[0], ret_recv.at[i], r_ssem.at[0], r_rsem.at[i], mate_dev).wait_recv()
 
     lane1 = iota((1, HD), 1)
     starts = jnp.full((1, HD), 1 << 30, jnp.int32)
@@ -112,14 +127,52 @@
     g_all[...] = jnp.swapaxes(g_in[...], 0, 1)
     loads[3].wait()
     q_all[...] = jnp.swapaxes(o_in[...], 0, 1)
+    lane_slot = jnp.where(lane1 >= DOC_LANE, lax.rem(lane1, 16), -1)
+    delta = jnp.zeros((TOK, HD), F32)
     for h in range(2 * GROUP):
         g = g_all[h].astype(F32)
-        go = g * q_all[h].astype(F32)
-        hi = go.astype(BF16)
-        cols = pl.ds(h * HD, HD)
-        go_hi[:, cols] = hi
-        go_lo[:, cols] = (go - hi.astype(F32)).astype(BF16)
+        summed = jnp.sum(g * q_all[h].astype(F32), axis=1, keepdims=True)
+        delta = jnp.where(lane_slot == h, summed, delta)
         g_all[h] = (g * scale).astype(BF16)
+
+    pl.semaphore_wait(barrier, greeted)
+
+    started = []
+
+    def start(there, copy):
+        @pl.when(there)
+        def _():
+            copy.start()
+        started.append((there, copy))
+
+    send_kv = remote(kv_send.at[1 - core], kvs.at[4 + core], kv_ssem.at[0], kv_rsem.at[4 + core], mate_dev)
+    send_kv.start()
+    for h in (0, 1):
+        start(after[1], remote(kv_send.at[h], kvs.at[2 + core], kv_ssem.at[1 + h], kv_rsem.at[2 + core], at(1, h)))
+
+    def arrive(there, landed, copy):
+        @pl.when(there)
+        def _():
+            copy.wait_recv()
+
+        @pl.when(jnp.logical_not(there))
+        def _():
+            landed[...] = jnp.zeros(landed.shape, landed.dtype)
+
+    def wait_block(kb):
+        arrive(before[2 - kb // 2], kvs.at[kb],
+               remote(kv_send.at[0], kvs.at[kb], kv_ssem.at[0], kv_rsem.at[kb], mate_dev))
+
+    def wait_return(i):
+        arrive(after[1 + i // 2], ret_recv.at[i],
+               remote(ret_send.at[0], ret_recv.at[i], r_ssem.at[0], r_rsem.at[i], mate_dev))
+
+    def wait_mate():
+        remote(kv_send.at[0], kvs.at[5 - core], kv_ssem.at[0], kv_rsem.at[5 - core], mate_dev).wait_recv()
+
+    for h in (0, 1):
+        start(hop_from_here, remote(kv_send.at[h], hop, hop_ssem.at[h], hop_rsem.at[0], (2 * down + h, tp)))
+
     send_g = remote(g_all.at[pl.ds(GROUP * (1 - core), GROUP)], g_s.at[core], x_ssem.at[0], x_rsem.at[0], mate_dev)
     send_g.start()
     loads[4].wait()
@@ -129,10 +182,6 @@
     g_s[core] = g_all[pl.ds(GROUP * core, GROUP)]
     q_s[core] = q_all[pl.ds(GROUP * core, GROUP)]
 
-    big = iota((2 * GROUP * HD, HD), 0) // HD
-    bl = iota((2 * GROUP * HD, HD), 1)
-    pick = jnp.where((bl >= DOC_LANE) & (bl < DOC_LANE + 48) & (lax.rem(bl, 16) == big), 1.0, 0.0).astype(BF16)
-    delta = dot(go_hi[...], pick, NN) + dot(go_lo[...], pick, NN)
     loads[5].wait()
     ln = ln_in[...]
     norm = jnp.concatenate([ln, ln, ln, jnp.zeros((80, TOK), F32)], axis=0).T
@@ -194,12 +243,17 @@
         return dot(qt[:, r], d_buf[r, c], NN), dot(gt[:, r], p_buf[r, c], NN)
 
     prepare(core)
-    wait_block(5 - core)
+    wait_mate()
     for s in (send_g, send_q, send_a):
         s.wait_recv()
     prepare(1 - core)
 
     scores(0, (4,), True)
+
+    @pl.when(hop_through_here)
+    def _():
+        remote(kv_send.at[0], hop, hop_ssem.at[0], hop_rsem.at[0], mate_dev).wait_recv()
+    start(hop_through_here, remote(hop, kvs.at[1], kv_ssem.at[4], kv_rsem.at[1], (2 * hop_end + core, tp)))
     scores(1, (4, 5), True)
     dk0, dv0 = kv_grads(0, 4, 1)
     dk1, dv1 = kv_grads(half, 5, 1)
@@ -210,53 +264,46 @@
     send_m = remote(own_part.at[1 - core], mate_part, m_ssem.at[0], m_rsem.at[0], mate_dev)
     send_m.start()
 
-    for j in (0, 1):
-        wait_block(2 + j)
-        onward = remote(kvs.at[2 + j], kvs.at[j], kv_ssem.at[3 + j], kv_rsem.at[j], at(1, core))
-        onward.start()
-        sends.append(onward)
-
-    returns = []
-
-    def give_back(i, j, chips, slot, dk, dv):
+    def pass_on(j):
+        start(before[1] & after[1],
+              remote(kvs.at[2 + j], kvs.at[j], kv_ssem.at[3 + j], kv_rsem.at[j], at(1, core)))
+
+    def give_back(i, j, chips, dk, dv):
         ret_send[i, 0] = dk.astype(BF16)
         ret_send[i, 1] = dv.astype(BF16)
-        c = remote(ret_send.at[i], ret_recv.at[slot + core], r_ssem.at[i], r_rsem.at[slot + core], at(chips, j))
-        c.start()
-        returns.append(c)
-
-    scores(0, (2, 3))
-    scores(1, (2, 3))
-    dk, dv = kv_grads(0, 2, 2)
-    for j in (0, 1):
-        give_back(j, j, -1, 0, dk[:, j * TOK:(j + 1) * TOK], dv[:, j * TOK:(j + 1) * TOK])
-
-    def query_grads(qb, first, count):
-        keys = kvs[first:first + count, 0].reshape(count * TOK, HD)
-        return dot(d_buf[qb * half:(qb + 1) * half, first * TOK:(first + count) * TOK], keys, NN)
-
-    dq_acc[0] = query_grads(0, 2, 3).reshape(GROUP, TOK, HD)
-    dq_acc[1] = query_grads(1, 2, 4).reshape(GROUP, TOK, HD)
-
+        slot = 2 * chips - 2 + core
+        start(before[chips], remote(ret_send.at[i], ret_recv.at[slot], r_ssem.at[i], r_rsem.at[slot], at(-chips, j)))
+
+    wait_block(2)
+    pass_on(0)
+    wait_block(3)
+    for j in (1, 0):
+        scores(0, (2 + j,))
+        scores(1, (2 + j,))
+        give_back(j, j, 1, *kv_grads(0, 2 + j, 1))
+
+    wait_block(1)
+    scores(0, (1,))
+    scores(1, (1,))
+    give_back(3, 1, 2, *kv_grads(0, 1, 1))
     wait_block(0)
     scores(0, (0,))
     r0 = pl.ds(0, half)
     c0 = pl.ds(0, TOK)
-    give_back(2, 0, -2, 2, dot(qt[:, r0], d_buf[r0, c0], NN), dot(gt[:, r0], p_buf[r0, c0], NN))
-    wait_block(1)
-    scores(0, (1,))
-    scores(1, (1,))
-    give_back(3, 1, -2, 2, *kv_grads(0, 1, 1))
-
-    dq_acc[0] = (dq_acc[0] + query_grads(0, 0, 2).reshape(GROUP, TOK, HD)) * SCALE
-    dq_acc[1] = (dq_acc[1] + query_grads(1, 1, 1).reshape(GROUP, TOK, HD)) * SCALE
-    send_dq = remote(dq_acc.at[1 - core], dq_mate, dq_ssem.at[0], dq_rsem.at[0], mate_dev)
+    give_back(2, 0, 2, dot(qt[:, r0], d_buf[r0, c0], NN), dot(gt[:, r0], p_buf[r0, c0], NN))
+
+    def query_grads(qb):
+        keys = kvs[pl.ds(qb, 5), 0].reshape(5 * TOK, HD)
+        r = pl.ds(pl.multiple_of(qb * half, half), half)
+        c = pl.ds(pl.multiple_of(qb * TOK, TOK), 5 * TOK)
+        return (dot(d_buf[r, c], keys, NN) * SCALE).reshape(GROUP, TOK, HD)
+
+    dq_send[...] = query_grads(1 - core)
+    send_dq = remote(dq_send, dq_all.at[pl.ds(GROUP * core, GROUP)], dq_ssem.at[0], dq_rsem.at[0], mate_dev)
     send_dq.start()
+    dq_all[pl.ds(GROUP * core, GROUP)] = query_grads(core)
     send_dq.wait_recv()
-    low = jnp.where(core == 0, dq_acc[core], dq_mate[...])
-    high = jnp.where(core == 0, dq_mate[...], dq_acc[core])
-    dq_ref[:, :GROUP] = jnp.swapaxes(low, 0, 1)
-    dq_ref[:, GROUP:] = jnp.swapaxes(high, 0, 1)
+    dq_ref[...] = jnp.swapaxes(dq_all[...], 0, 1)
 
     send_m.wait_recv()
     for i in range(4):
@@ -271,8 +318,10 @@
     add_up(mate_part[...], 1 - core)
     dk_ref[...] = jnp.swapaxes(totals[0], 0, 1)
     dv_ref[...] = jnp.swapaxes(totals[1], 0, 1)
-    for s in sends + [send_g, send_q, send_a, send_m, send_dq] + returns:
+    for s in (send_kv, send_g, send_q, send_a, send_m, send_dq):
         s.wait_send()
+    for there, copy in started:
+        pl.when(there)(copy.wait_send)
 
 
 def shards(n_ctx, queries, keys, values, attn_out, grad_out, log_norm, doc_lengths, doc_weight):
@@ -301,13 +350,13 @@
             buf(2 * GROUP, TOK, HD), buf(2 * GROUP, TOK, HD), buf(TOK, HD),
             buf(2, GROUP, TOK, HD), buf(2, GROUP, TOK, HD), buf(2, TOK, HD),
             buf(2, GROUP, TOK, HD), buf(2, GROUP, TOK, HD),
-            buf(HD, wide), buf(HD, wide), buf(TOK, 2 * GROUP * HD), buf(TOK, 2 * GROUP * HD),
+            buf(HD, wide), buf(HD, wide),
             buf(wide, 6 * TOK), buf(wide, 6 * TOK),
             buf(2, 2, HD, TOK, dtype=F32), buf(2, HD, TOK, dtype=F32),
             buf(4, 2, HD, TOK), buf(4, 2, HD, TOK),
-            buf(2, GROUP, TOK, HD, dtype=F32), buf(GROUP, TOK, HD, dtype=F32), buf(2, 2, TOK, HD, dtype=F32),
+            buf(GROUP, TOK, HD, dtype=F32), buf(2 * GROUP, TOK, HD, dtype=F32), buf(2, 2, TOK, HD, dtype=F32),
             dma((6,)), dma((5,)), dma((6,)), dma((3,)), dma((3,)), dma((4,)), dma((4,)), dma((1,)), dma((1,)),
-            dma((1,)), dma((1,)),
+            dma((1,)), dma((1,)), buf(2, TOK, HD), dma((2,)), dma((1,)),
         ],
         compiler_params=pltpu.CompilerParams(collective_id=0, has_side_effects=True, vmem_limit_bytes=52 << 20),
     )(queries, keys, values, attn_out, grad_out, log_norm, doc_lengths, doc_weight)

time: 38.3 us -> 33.2 us (0.87)
  the two profiles are of different devices: /device:TPU:1 before, /device:TPU:112 now
where the time goes in v3:
time: 33.2 us; the launch traced here: 33.1 us
  Pallas kernels  29.8 us (90%)
  local copies, waits for them, and re-layouts  2.73 us (8%)
  between operations  0.64 us (2%)
    pallas_call x1, Pallas kernels, shards(): pl.pallas_call(functools.partial(kernel, n_ctx), out_shape=(buf(*q_shape,...  29.8 us
    unnamed x3, local copies, waits for them, and re-layouts  2.73 us

profile of v3, /device:TPU:112, one launch (start us, length us, event | category | flops | bytes accessed | tf_op | source)
XLA Modules:
  0.0 33.1 jit_solution(10917189917994718960)
XLA Ops:
  0.6 29.8 %shard_map.103 = (f32[256,16,128]{2,1,0:T(8,128)S(1)}, f32[256,2,128]{2,1,0:T(2,128)S(1)}, f32[256,2,128]{2,1,0:T(2,128)S(1)}) custom-call(bf16[256,16,128]{2,1,0:T(8,128)(2,1)} %q_hbm.1, bf16[256,2,128]{2,1,0:T(2,128)(2,1)} %k_hbm.1, bf16[256,2,128]{2,1,0:T(2,128)(2,1)} %v_hbm.1, bf16[256,16,128]{2,1,0:T(8,128)(2,1)} %o_hbm.1, bf16[256,16,128]{2,1,0:T(8,128)(2,1)} %g_hbm.1, ...), custom_call_target="tpu_custom_call" | custom-call | tf_op jit(solution)/shard_map/pallas_call | solution.py:338
  30.4 1.3 %copy.14 = f32[256,16,128]{2,1,0:T(8,128)} copy(f32[256,16,128]{2,1,0:T(8,128)S(1)} %get-tuple-element.3) | data formatting | bytes 4194304
  31.7 0.7 %copy.15 = f32[256,2,128]{2,1,0:T(2,128)} copy(f32[256,2,128]{2,1,0:T(2,128)S(1)} %get-tuple-element.4) | data formatting | bytes 524288
  32.4 0.7 %copy.16 = f32[256,2,128]{2,1,0:T(2,128)} copy(f32[256,2,128]{2,1,0:T(2,128)S(1)} %get-tuple-element.5) | data formatting | bytes 524288

commit v4 on v3

--- a/solution.py
+++ b/solution.py
@@ -17,6 +17,7 @@
 GROUP = 8
 DOCS = 32
 RING = 4
+PIECES = 2
 SCALE = HD ** -0.5
 DOC_LANE = 64
 FAR_AWAY = 16384.0
@@ -30,10 +31,10 @@
     return lax.broadcasted_iota(jnp.int32, shape, dim)
 
 
-def kernel(n_ctx, q_hbm, k_hbm, v_hbm, o_hbm, g_hbm, ln_hbm, dl_ref, dw_ref, dq_ref, dk_ref, dv_ref,
+def kernel(n_ctx, q_hbm, k_hbm, v_hbm, o_hbm, g_hbm, ln_hbm, dl_ref, dw_ref, dq_ref, dkv_ref,
            q_in, k_in, v_in, o_in, g_in, ln_in,
            kv_send, kvs, kaug, q_all, g_all, a_all, q_s, g_s, a_s, xaug, yaug, qt, gt,
-           p_buf, d_buf, own_part, mate_part, ret_send, ret_recv, dq_send, dq_all, totals,
+           p_buf, d_buf, own_part, mate_part, ret_send, ret_recv, dq_send, dq_recv, totals,
            in_sem, kv_ssem, kv_rsem, x_ssem, x_rsem, r_ssem, r_rsem, m_ssem, m_rsem, dq_ssem, dq_rsem, hop, hop_ssem, hop_rsem):
     me = lax.axis_index("ctx")
     tp = lax.axis_index("tp")
@@ -62,8 +63,8 @@
     mate_dev = (mate, tp)
     loads = [pltpu.make_async_copy(s, d, in_sem.at[i]) for i, (s, d) in enumerate(
         [(k_hbm, k_in), (v_hbm, v_in), (g_hbm, g_in), (o_hbm, o_in), (q_hbm, q_in), (ln_hbm, ln_in)])]
-    for load in loads:
-        load.start()
+    loads[0].start()
+    loads[1].start()
     barrier = pltpu.get_barrier_semaphore()
     pl.semaphore_signal(barrier, inc=1, device_id=mate_dev, device_id_type=MESH)
     greeted = 1
@@ -85,6 +86,8 @@
             for dev in devs:
                 pl.semaphore_signal(barrier, inc=1, device_id=dev, device_id_type=MESH)
 
+    for load in loads[2:]:
+        load.start()
     loads[0].wait()
     kv_send[:, 0] = jnp.swapaxes(k_in[...], 0, 1)
     loads[1].wait()
@@ -147,8 +150,13 @@
 
     send_kv = remote(kv_send.at[1 - core], kvs.at[4 + core], kv_ssem.at[0], kv_rsem.at[4 + core], mate_dev)
     send_kv.start()
-    for h in (0, 1):
-        start(after[1], remote(kv_send.at[h], kvs.at[2 + core], kv_ssem.at[1 + h], kv_rsem.at[2 + core], at(1, h)))
+
+    def send_near(j):
+        for h in (0, 1):
+            start(after[1] & (core == j),
+                  remote(kv_send.at[h], kvs.at[2 + core], kv_ssem.at[1 + h], kv_rsem.at[2 + core], at(1, h)))
+
+    send_near(0)
 
     def arrive(there, landed, copy):
         @pl.when(there)
@@ -221,17 +229,16 @@
 
     def scores(qb, kbs, diagonal=False):
         width = TOK * len(kbs)
-        cols = pl.ds(kbs[0] * TOK, width)
+        cols = pl.ds(pl.multiple_of(kbs[0] * TOK, TOK), width)
         keys, values = keys_of(kbs), values_of(kbs)
         for g in range(GROUP):
             x = jnp.concatenate([q_s[qb, g], xaug[qb, g]], axis=1)
             y = jnp.concatenate([g_s[qb, g], yaug[qb, g]], axis=1)
             p = jnp.exp(dot(x, keys, NT) * SCALE)
             if diagonal:
-                keep = causal if len(kbs) == 1 else jnp.concatenate([jnp.ones((TOK, TOK), jnp.bool_), causal], axis=1)
-                p = jnp.where(keep, p, 0.0)
+                p = jnp.where(causal, p, 0.0)
             ds = p * dot(y, values, NT)
-            at_rows = pl.ds((qb * GROUP + g) * TOK, TOK)
+            at_rows = pl.ds(pl.multiple_of((qb * GROUP + g) * TOK, TOK), TOK)
             p_buf[at_rows, cols] = p.astype(BF16)
             d_buf[at_rows, cols] = ds.astype(BF16)
 
@@ -243,26 +250,27 @@
         return dot(qt[:, r], d_buf[r, c], NN), dot(gt[:, r], p_buf[r, c], NN)
 
     prepare(core)
+    scores(core, (4 + core,), True)
     wait_mate()
     for s in (send_g, send_q, send_a):
         s.wait_recv()
     prepare(1 - core)
-
-    scores(0, (4,), True)
+    send_near(1)
+
+    scores(1 - core, (5 - core,), True)
+    scores(1, (4,))
 
     @pl.when(hop_through_here)
     def _():
         remote(kv_send.at[0], hop, hop_ssem.at[0], hop_rsem.at[0], mate_dev).wait_recv()
     start(hop_through_here, remote(hop, kvs.at[1], kv_ssem.at[4], kv_rsem.at[1], (2 * hop_end + core, tp)))
-    scores(1, (4, 5), True)
-    dk0, dv0 = kv_grads(0, 4, 1)
-    dk1, dv1 = kv_grads(half, 5, 1)
-    own_part[0, 0] = dk0
-    own_part[0, 1] = dv0
-    own_part[1, 0] = dk1
-    own_part[1, 1] = dv1
-    send_m = remote(own_part.at[1 - core], mate_part, m_ssem.at[0], m_rsem.at[0], mate_dev)
-    send_m.start()
+
+    def own_grads(j):
+        dk, dv = kv_grads(j * half, 4 + j, 1)
+        own_part[j, 0] = dk
+        own_part[j, 1] = dv
+
+    own_grads(0)
 
     def pass_on(j):
         start(before[1] & after[1],
@@ -274,10 +282,11 @@
         slot = 2 * chips - 2 + core
         start(before[chips], remote(ret_send.at[i], ret_recv.at[slot], r_ssem.at[i], r_rsem.at[slot], at(-chips, j)))
 
-    wait_block(2)
-    pass_on(0)
-    wait_block(3)
-    for j in (1, 0):
+    send_m = remote(own_part.at[1 - core], mate_part, m_ssem.at[0], m_rsem.at[0], mate_dev)
+    for j in (0, 1):
+        wait_block(2 + j)
+        if j == 0:
+            pass_on(0)
         scores(0, (2 + j,))
         scores(1, (2 + j,))
         give_back(j, j, 1, *kv_grads(0, 2 + j, 1))
@@ -292,18 +301,28 @@
     c0 = pl.ds(0, TOK)
     give_back(2, 0, 2, dot(qt[:, r0], d_buf[r0, c0], NN), dot(gt[:, r0], p_buf[r0, c0], NN))
 
-    def query_grads(qb):
+    def query_grads(qb, i):
         keys = kvs[pl.ds(qb, 5), 0].reshape(5 * TOK, HD)
-        r = pl.ds(pl.multiple_of(qb * half, half), half)
+        r = pl.ds(pl.multiple_of(qb * half + i * (half // PIECES), half // PIECES), half // PIECES)
         c = pl.ds(pl.multiple_of(qb * TOK, TOK), 5 * TOK)
-        return (dot(d_buf[r, c], keys, NN) * SCALE).reshape(GROUP, TOK, HD)
-
-    dq_send[...] = query_grads(1 - core)
-    send_dq = remote(dq_send, dq_all.at[pl.ds(GROUP * core, GROUP)], dq_ssem.at[0], dq_rsem.at[0], mate_dev)
-    send_dq.start()
-    dq_all[pl.ds(GROUP * core, GROUP)] = query_grads(core)
-    send_dq.wait_recv()
-    dq_ref[...] = jnp.swapaxes(dq_all[...], 0, 1)
+        return (dot(d_buf[r, c], keys, NN) * SCALE).reshape(GROUP // PIECES, TOK, HD)
+
+    sends_dq = []
+    for i in range(PIECES):
+        dq_send[i] = query_grads(1 - core, i)
+        c = remote(dq_send.at[i], dq_recv.at[i], dq_ssem.at[i], dq_rsem.at[i], mate_dev)
+        c.start()
+        sends_dq.append(c)
+    own_grads(1)
+    send_m.start()
+
+    def put(group, x):
+        dq_ref[:, pl.ds(pl.multiple_of(GROUP * group, GROUP), GROUP)] = jnp.swapaxes(x, 0, 1)
+
+    put(core, jnp.concatenate([query_grads(core, i) for i in range(PIECES)], axis=0))
+    for c in sends_dq:
+        c.wait_recv()
+    put(1 - core, dq_recv[...].reshape(GROUP, TOK, HD))
 
     send_m.wait_recv()
     for i in range(4):
@@ -316,9 +335,9 @@
 
     add_up(own_part[core], core)
     add_up(mate_part[...], 1 - core)
-    dk_ref[...] = jnp.swapaxes(totals[0], 0, 1)
-    dv_ref[...] = jnp.swapaxes(totals[1], 0, 1)
-    for s in (send_kv, send_g, send_q, send_a, send_m, send_dq):
+    dkv_ref[0] = jnp.swapaxes(totals[0], 0, 1)
+    dkv_ref[1] = jnp.swapaxes(totals[1], 0, 1)
+    for s in [send_kv, send_g, send_q, send_a, send_m] + sends_dq:
         s.wait_send()
     for there, copy in started:
         pl.when(there)(copy.wait_send)
@@ -335,15 +354,14 @@
     def buf(*shape, dtype=BF16):
         return pltpu.VMEM(shape, dtype)
 
-    return pl.pallas_call(
+    dq, dkv = pl.pallas_call(
         functools.partial(kernel, n_ctx),
         out_shape=(
             buf(*q_shape, dtype=F32),
-            buf(*k_shape, dtype=F32),
-            buf(*k_shape, dtype=F32),
+            buf(2, *k_shape, dtype=F32),
         ),
         in_specs=[any_space] * 6 + [smem] * 2,
-        out_specs=(vmem, vmem, vmem),
+        out_specs=(vmem, vmem),
         scratch_shapes=[
             buf(*q_shape), buf(*k_shape), buf(*k_shape), buf(*q_shape), buf(*q_shape), buf(2 * GROUP, TOK, dtype=F32),
             buf(2, 2, TOK, HD), buf(6, 2, TOK, HD), buf(6, TOK, HD),
@@ -354,12 +372,14 @@
             buf(wide, 6 * TOK), buf(wide, 6 * TOK),
             buf(2, 2, HD, TOK, dtype=F32), buf(2, HD, TOK, dtype=F32),
             buf(4, 2, HD, TOK), buf(4, 2, HD, TOK),
-            buf(GROUP, TOK, HD, dtype=F32), buf(2 * GROUP, TOK, HD, dtype=F32), buf(2, 2, TOK, HD, dtype=F32),
+            buf(PIECES, GROUP // PIECES, TOK, HD, dtype=F32), buf(PIECES, GROUP // PIECES, TOK, HD, dtype=F32),
+            buf(2, 2, TOK, HD, dtype=F32),
             dma((6,)), dma((5,)), dma((6,)), dma((3,)), dma((3,)), dma((4,)), dma((4,)), dma((1,)), dma((1,)),
-            dma((1,)), dma((1,)), buf(2, TOK, HD), dma((2,)), dma((1,)),
+            dma((PIECES,)), dma((PIECES,)), buf(2, TOK, HD), dma((2,)), dma((1,)),
         ],
         compiler_params=pltpu.CompilerParams(collective_id=0, has_side_effects=True, vmem_limit_bytes=52 << 20),
     )(queries, keys, values, attn_out, grad_out, log_norm, doc_lengths, doc_weight)
+    return dq, dkv[0], dkv[1]
 
 
 def solution(mesh):

time: 33.2 us -> 31.4 us (0.946)
  Pallas kernels: 29.8 us -> 28.5 us
  local copies, waits for them, and re-layouts: 2.73 us -> 2.14 us
    unnamed x3 -> x1, local copies, waits for them, and re-layouts: 2.73 us -> 1.32 us
    pallas_call x1, Pallas kernels: 29.8 us -> 28.5 us  [shards(): pl.pallas_call(functools.partial(kernel, n_ctx), out_shape=(buf(*q_shape,...]
    squeeze x0 -> x1, local copies, waits for them, and re-layouts: none -> 0.82 us  [shards(): return (dq, dkv[0], dkv[1])]
where the time goes in v4:
time: 31.4 us; the launch traced here: 31.3 us
  Pallas kernels  28.5 us (91%)
  local copies, waits for them, and re-layouts  2.14 us (7%)
  between operations  0.64 us (2%)
    pallas_call x1, Pallas kernels, shards(): pl.pallas_call(functools.partial(kernel, n_ctx), out_shape=(buf(*q_shape,...  28.5 us
    unnamed x1, local copies, waits for them, and re-layouts  1.32 us
    squeeze x1, local copies, waits for them, and re-layouts, shards(): return (dq, dkv[0], dkv[1])  0.82 us

profile of v4, /device:TPU:112, one launch (start us, length us, event | category | flops | bytes accessed | tf_op | source)
XLA Modules:
  0.0 31.3 jit_solution(10974649417974716938)
XLA Ops:
  0.6 28.5 %shard_map.103 = (f32[256,16,128]{2,1,0:T(8,128)S(1)}, f32[2,256,2,128]{3,2,1,0:T(2,128)S(1)}) custom-call(bf16[256,16,128]{2,1,0:T(8,128)(2,1)} %q_hbm.1, bf16[256,2,128]{2,1,0:T(2,128)(2,1)} %k_hbm.1, bf16[256,2,128]{2,1,0:T(2,128)(2,1)} %v_hbm.1, bf16[256,16,128]{2,1,0:T(8,128)(2,1)} %o_hbm.1, bf16[256,16,128]{2,1,0:T(8,128)(2,1)} %g_hbm.1, ...), custom_call_target="tpu_custom_call" | custom-call | tf_op jit(solution)/shard_map/pallas_call | solution.py:357
  29.2 1.3 %copy.12 = f32[256,16,128]{2,1,0:T(8,128)} copy(f32[256,16,128]{2,1,0:T(8,128)S(1)} %get-tuple-element.9) | data formatting | bytes 4194304
  30.5 0.8 %slice_bitcast_fusion = (f32[256,2,128]{2,1,0:T(2,128)}, f32[256,2,128]{2,1,0:T(2,128)}) fusion(f32[2,256,2,128]{3,2,1,0:T(2,128)S(1)} %get-tuple-element.6), kind=kLoop, calls=%fused_computation | loop fusion | bytes 1048576 | tf_op jit(solution)/shard_map/squeeze | solution.py:382

commit v5 on v4

--- a/solution.py
+++ b/solution.py
@@ -341,6 +341,15 @@
         s.wait_send()
     for there, copy in started:
         pl.when(there)(copy.wait_send)
+
+
+def write_out(dq_in, dkv_in, dq_ref, dk_ref, dv_ref, sems):
+    copies = [pltpu.make_async_copy(src, dst, sems.at[i])
+              for i, (src, dst) in enumerate(((dq_in, dq_ref), (dkv_in.at[0], dk_ref), (dkv_in.at[1], dv_ref)))]
+    for c in copies:
+        c.start()
+    for c in copies:
+        c.wait()
 
 
 def shards(n_ctx, queries, keys, values, attn_out, grad_out, log_norm, doc_lengths, doc_weight):
@@ -379,7 +388,16 @@
         ],
         compiler_params=pltpu.CompilerParams(collective_id=0, has_side_effects=True, vmem_limit_bytes=52 << 20),
     )(queries, keys, values, attn_out, grad_out, log_norm, doc_lengths, doc_weight)
-    return dq, dkv[0], dkv[1]
+    dq = pltpu.with_memory_space_constraint(dq, pltpu.VMEM)
+    dkv = pltpu.with_memory_space_constraint(dkv, pltpu.VMEM)
+    return pl.pallas_call(
+        write_out,
+        out_shape=tuple(jax.ShapeDtypeStruct(shape, F32) for shape in (q_shape, k_shape, k_shape)),
+        in_specs=[vmem] * 2,
+        out_specs=(any_space,) * 3,
+        scratch_shapes=[dma((3,))],
+        compiler_params=pltpu.CompilerParams(vmem_limit_bytes=16 << 20),
+    )(dq, dkv)
 
 
 def solution(mesh):

time: 31.4 us -> 30.9 us (0.984)
  local copies, waits for them, and re-layouts: 2.14 us -> 0 us
  Pallas kernels: 28.5 us -> 30 us
    pallas_call x0 -> x1, Pallas kernels: none -> 1.51 us  [shards(): pl.pallas_call(write_out, out_shape=tuple((jax.ShapeDtypeStruct(shape, F3...]
    unnamed x1 -> x0, local copies, waits for them, and re-layouts: 1.32 us -> none
    squeeze x1 -> x0, local copies, waits for them, and re-layouts: 0.82 us -> none  [shards(): return (dq, dkv[0], dkv[1])]
where the time goes in v5:
time: 30.9 us; the launch traced here: 30.8 us
  Pallas kernels  30 us (97%)
  between operations  0.8 us (3%)
    pallas_call x1, Pallas kernels, shards(): pl.pallas_call(functools.partial(kernel, n_ctx), out_shape=(buf(*q_shape,...  28.5 us
    pallas_call x1, Pallas kernels, shards(): pl.pallas_call(write_out, out_shape=tuple((jax.ShapeDtypeStruct(shape, F3...  1.51 us

profile of v5, /device:TPU:112, one launch (start us, length us, event | category | flops | bytes accessed | tf_op | source)
XLA Modules:
  0.0 30.8 jit_solution(1713615506976244557)
XLA Ops:
  0.6 28.5 %shard_map.103 = (f32[256,16,128]{2,1,0:T(8,128)S(1)}, f32[2,256,2,128]{3,2,1,0:T(2,128)S(1)}) custom-call(bf16[256,16,128]{2,1,0:T(8,128)(2,1)} %q_hbm.1, bf16[256,2,128]{2,1,0:T(2,128)(2,1)} %k_hbm.1, bf16[256,2,128]{2,1,0:T(2,128)(2,1)} %v_hbm.1, bf16[256,16,128]{2,1,0:T(8,128)(2,1)} %o_hbm.1, bf16[256,16,128]{2,1,0:T(8,128)(2,1)} %g_hbm.1, ...), custom_call_target="tpu_custom_call" | custom-call | tf_op jit(solution)/shard_map/pallas_call | solution.py:366
  29.2 1.5 %shard_map.104 = (f32[256,16,128]{2,1,0:T(8,128)}, f32[256,2,128]{2,1,0:T(2,128)}, f32[256,2,128]{2,1,0:T(2,128)}) custom-call(f32[256,16,128]{2,1,0:T(8,128)S(1)} %get-tuple-element.5.dq_in, f32[2,256,2,128]{3,2,1,0:T(2,128)S(1)} %get-tuple-element.6.dkv_in), custom_call_target="tpu_custom_call" | custom-call | tf_op jit(solution)/shard_map/pallas_call | solution.py:393

commit v6 on v5

--- a/solution.py
+++ b/solution.py
@@ -270,11 +270,13 @@
         own_part[j, 0] = dk
         own_part[j, 1] = dv
 
-    own_grads(0)
-
     def pass_on(j):
         start(before[1] & after[1],
               remote(kvs.at[2 + j], kvs.at[j], kv_ssem.at[3 + j], kv_rsem.at[j], at(1, core)))
+
+    wait_block(2)
+    pass_on(0)
+    own_grads(0)
 
     def give_back(i, j, chips, dk, dv):
         ret_send[i, 0] = dk.astype(BF16)
@@ -284,9 +286,8 @@
 
     send_m = remote(own_part.at[1 - core], mate_part, m_ssem.at[0], m_rsem.at[0], mate_dev)
     for j in (0, 1):
-        wait_block(2 + j)
-        if j == 0:
-            pass_on(0)
+        if j == 1:
+            wait_block(3)
         scores(0, (2 + j,))
         scores(1, (2 + j,))
         give_back(j, j, 1, *kv_grads(0, 2 + j, 1))

time: 30.9 us -> 31.5 us (1.019)
  Pallas kernels: 30 us -> 30.6 us
    pallas_call x1, Pallas kernels: 28.5 us -> 29.1 us  [shards(): pl.pallas_call(functools.partial(kernel, n_ctx), out_shape=(buf(*q_shape,...]
where the time goes in v6:
time: 31.5 us; the launch traced here: 31.4 us
  Pallas kernels  30.6 us (97%)
  between operations  0.8 us (3%)
    pallas_call x1, Pallas kernels, shards(): pl.pallas_call(functools.partial(kernel, n_ctx), out_shape=(buf(*q_shape,...  29.1 us
    pallas_call x1, Pallas kernels, shards(): pl.pallas_call(write_out, out_shape=tuple((jax.ShapeDtypeStruct(shape, F3...  1.51 us

profile of v6, /device:TPU:112, one launch (start us, length us, event | category | flops | bytes accessed | tf_op | source)
XLA Modules:
  0.0 31.4 jit_solution(12852921620612634534)
XLA Ops:
  0.6 29.1 %shard_map.103 = (f32[256,16,128]{2,1,0:T(8,128)S(1)}, f32[2,256,2,128]{3,2,1,0:T(2,128)S(1)}) custom-call(bf16[256,16,128]{2,1,0:T(8,128)(2,1)} %q_hbm.1, bf16[256,2,128]{2,1,0:T(2,128)(2,1)} %k_hbm.1, bf16[256,2,128]{2,1,0:T(2,128)(2,1)} %v_hbm.1, bf16[256,16,128]{2,1,0:T(8,128)(2,1)} %o_hbm.1, bf16[256,16,128]{2,1,0:T(8,128)(2,1)} %g_hbm.1, ...), custom_call_target="tpu_custom_call" | custom-call | tf_op jit(solution)/shard_map/pallas_call | solution.py:367
  29.7 1.5 %shard_map.104 = (f32[256,16,128]{2,1,0:T(8,128)}, f32[256,2,128]{2,1,0:T(2,128)}, f32[256,2,128]{2,1,0:T(2,128)}) custom-call(f32[256,16,128]{2,1,0:T(8,128)S(1)} %get-tuple-element.5.dq_in, f32[2,256,2,128]{3,2,1,0:T(2,128)S(1)} %get-tuple-element.6.dkv_in), custom_call_target="tpu_custom_call" | custom-call | tf_op jit(solution)/shard_map/pallas_call | solution.py:394
